TPU v7x, 128 devices: a whole 4x4x4 slice. The times are simulated.
128 devices in a mesh: seq: 16 (over x, y), pipe: 8 (over z, core).
Axes of the slice: x: 4, y: 4, z: 4, core: 2. Of those that a mesh axis runs over, the one named last changes fastest.
Arguments:
- query_in: bfloat16 [8, 2048, 4096], P('pipe', 'seq'), may hold values from -6 to 6
- key_in: bfloat16 [8, 2048, 4096], P('pipe', 'seq'), may hold values from -6 to 6
- value_in: bfloat16 [8, 2048, 4096], P('pipe', 'seq'), may hold values from -6 to 6
- grad_out: bfloat16 [8, 2048, 4096], P('pipe', 'seq'), may hold values from -6 to 6
- long_filter: float32 [8, 2048, 256], P('pipe', 'seq'), may hold values from -2 to 2, as said below
- short_taps: float32 [8, 3, 3, 4096], P('pipe'), may hold values from -3 to 3
Outputs:
- layer_out: bfloat16 [8, 2048, 4096], P('pipe', 'seq')
- passed_grads: bfloat16 [8, 3, 2048, 4096], P('pipe', None, 'seq')
- filter_grad: float32 [8, 2048, 256], P('pipe', 'seq')
- tap_grads: float32 [8, 3, 3, 4096], P('pipe')
Inputs may be any that keep to these rules, and one draw needn't show every extreme that they name: `long_filter`: one filter for each channel group of each section.
All inputs are finite; a program needn't handle non-finite values.
Results may differ from a plain program's by a relative error of at most 0.005.
Values may be sent and summed in bfloat16 or wider, within the bound.
A program may use at most 256 MiB of HBM per device.

v0:
```python
import math

import jax
import jax.numpy as jnp
from jax import lax
from jax.sharding import PartitionSpec as P

exact_mode = lax.Precision.HIGHEST


def passed_along(x, axis, by):
    count = lax.axis_size(axis)
    pairs = [(i, i + by) for i in range(count) if 0 <= i + by < count]
    return lax.ppermute(x, axis, pairs)


def counting(length):
    return jnp.arange(length, dtype=jnp.int32)


def matmul(left, right):
    return jnp.dot(left, right, precision=exact_mode, preferred_element_type=jnp.float32)


def phases(row_index, col_index, modulus, direction):
    index_product = row_index[:, None] * col_index[None, :] % modulus
    phase_angle = index_product.astype(jnp.float32) * (-2.0 * math.pi * direction / modulus)
    return (jnp.cos(phase_angle), jnp.sin(phase_angle))


def complex_table(row_index, col_index, modulus, direction, factor):
    cosine_part, sine_part = phases(row_index, col_index, modulus, direction)
    upper = jnp.concatenate([cosine_part, -sine_part], axis=1)
    lower = jnp.concatenate([sine_part, cosine_part], axis=1)
    return jnp.concatenate([upper, lower], axis=0) * factor


def lead_segment(packed, row_index, col_index, modulus, direction, factor):
    in_shape = packed.shape
    flattened = packed.reshape(2 * in_shape[1], -1)
    table = complex_table(row_index, col_index, modulus, direction, factor)
    joined = matmul(table, flattened)
    return joined.reshape((2, row_index.shape[0]) + in_shape[2:])


def middle_segment(packed, row_index, col_index, modulus, direction):
    table = complex_table(row_index, col_index, modulus, direction, 1.0)
    table = table.reshape(2, row_index.shape[0], 2, col_index.shape[0])
    return jnp.einsum(
        "xrzb,zkbw->xkrw", table, packed, precision=exact_mode, preferred_element_type=jnp.float32
    )


def twiddle(packed, row_index, col_index, modulus, direction):
    cosine_part, sine_part = phases(row_index, col_index, modulus, direction)
    cosine_part = cosine_part[:, :, None]
    sine_part = sine_part[:, :, None]
    return jnp.stack(
        [
            packed[0] * cosine_part - packed[1] * sine_part,
            packed[0] * sine_part + packed[1] * cosine_part,
        ]
    )


def pack_pairs(values, pack_block):
    lead_dims = values.shape[:-1]
    split_view = values.reshape(lead_dims + (values.shape[-1] // (2 * pack_block), 2, pack_block))
    return jnp.stack(
        [
            split_view[..., 0, :].reshape(lead_dims + (-1,)),
            split_view[..., 1, :].reshape(lead_dims + (-1,)),
        ]
    )


def unpack_pairs(packed, pack_block):
    lead_dims = packed.shape[1:-1]
    pair_view = packed.reshape((2,) + lead_dims + (packed.shape[-1] // pack_block, pack_block))
    joined = jnp.stack([pair_view[0], pair_view[1]], axis=-2)
    return joined.reshape(lead_dims + (-1,))


def group_table(first_packed, col_count, half_group, groups):
    packed_index = first_packed + counting(col_count)
    return (packed_index[None, :] // half_group == counting(groups)[:, None]).astype(jnp.float32)


def spec_product(first_spec, second_spec):
    return jnp.stack(
        [
            first_spec[0] * second_spec[0] - first_spec[1] * second_spec[1],
            first_spec[0] * second_spec[1] + first_spec[1] * second_spec[0],
        ]
    )


def conj_product(first_spec, second_spec):
    return jnp.stack(
        [
            first_spec[0] * second_spec[0] + first_spec[1] * second_spec[1],
            first_spec[1] * second_spec[0] - first_spec[0] * second_spec[1],
        ]
    )


def spread_groups(spectrum, group_map):
    return jnp.einsum(
        "rktg,gq->rktq",
        spectrum,
        group_map,
        precision=exact_mode,
        preferred_element_type=jnp.float32,
    )


def sum_groups(spectrum, group_map):
    return jnp.einsum(
        "rktq,gq->rktg",
        spectrum,
        group_map,
        precision=exact_mode,
        preferred_element_type=jnp.float32,
    )


def local(query_in, key_in, value_in, grad_out, long_filter, short_taps):
    seq_size = lax.axis_size("seq")
    seq_rank = lax.axis_index("seq")
    rows_dev = query_in.shape[1]
    width = query_in.shape[2]
    groups = long_filter.shape[2]
    half_group = width // groups // 2
    pack_block = half_group // 2
    total_rows = rows_dev * seq_size
    fft_length = 2 * total_rows
    tap_table = short_taps[0]
    stacked_in = jnp.stack([query_in[0], key_in[0], value_in[0]])
    before = passed_along(stacked_in[:, rows_dev - 2 :, :], "seq", 1)
    extended = jnp.concatenate([before, stacked_in], axis=1).astype(jnp.float32)
    featured = tap_table[:, 0, None, :] * extended[:, 2 : 2 + rows_dev, :]
    featured = featured + tap_table[:, 1, None, :] * extended[:, 1 : 1 + rows_dev, :]
    featured = featured + tap_table[:, 2, None, :] * extended[:, 0:rows_dev, :]
    query_feat = featured[0]
    keyed = featured[1]
    valued = featured[2]
    grad_float = grad_out[0].astype(jnp.float32)
    product = (keyed * valued).astype(jnp.bfloat16)
    scaled = (grad_float * query_feat).astype(jnp.bfloat16)
    block_rows = rows_dev // seq_size
    group_map = group_table(0, width // 2, half_group, groups)
    freq_index = (
        (2 * seq_rank + counting(2))[:, None] + 2 * seq_size * counting(rows_dev)[None, :]
    ).reshape(-1)
    whole_filter = lax.all_gather(long_filter[0], "seq", axis=0, tiled=True)
    filter_cos, filter_sin = phases(freq_index, counting(total_rows), fft_length, 1)
    own_spec = jnp.stack(
        [matmul(filter_cos, whole_filter), matmul(filter_sin, whole_filter)]
    ).reshape(2, 2, rows_dev, groups)
    kernel = spread_groups(own_spec, group_map)

    def forward(signal):
        arrived = lax.all_to_all(signal[None], "seq", split_axis=1, concat_axis=0, tiled=True)
        packed = pack_pairs(arrived.astype(jnp.float32), pack_block)
        first_segment = lead_segment(
            packed, counting(2 * seq_size), counting(seq_size), 2 * seq_size, 1, 1.0
        )
        turned = twiddle(
            first_segment,
            counting(2 * seq_size),
            seq_rank * block_rows + counting(block_rows),
            fft_length,
            1,
        )
        gathered = lax.all_to_all(turned, "seq", split_axis=1, concat_axis=2, tiled=True)
        return middle_segment(gathered, counting(rows_dev), counting(rows_dev), rows_dev, 1)

    def inverse(spectrum):
        back_segment = middle_segment(
            spectrum, counting(rows_dev), counting(rows_dev), rows_dev, -1
        )
        turned = twiddle(
            back_segment, 2 * seq_rank + counting(2), counting(rows_dev), fft_length, -1
        )
        arrived = lax.all_to_all(turned, "seq", split_axis=2, concat_axis=1, tiled=True)
        row_data = lead_segment(
            arrived, counting(seq_size), counting(2 * seq_size), 2 * seq_size, -1, 1.0 / fft_length
        )
        spread_back = unpack_pairs(row_data, pack_block)
        return lax.all_to_all(spread_back, "seq", split_axis=0, concat_axis=1, tiled=True)[0]

    prod_spec = forward(product)
    conv_out = inverse(spec_product(prod_spec, kernel))
    scaled_spec = forward(scaled)
    back_out = inverse(conj_product(scaled_spec, kernel))
    cross_spec = sum_groups(conj_product(scaled_spec, prod_spec), group_map)
    cross_real = cross_spec[0].reshape(2 * rows_dev, groups)
    cross_imag = cross_spec[1].reshape(2 * rows_dev, groups)
    layer_out = (query_feat * conv_out).astype(jnp.bfloat16)
    grad_stack = jnp.stack([grad_float * conv_out, back_out * valued, back_out * keyed])
    after_rows = passed_along(grad_stack[:, :2, :].astype(jnp.bfloat16), "seq", -1).astype(
        jnp.float32
    )
    padded = jnp.concatenate([grad_stack, after_rows], axis=1)
    input_grads = tap_table[:, 0, None, :] * padded[:, 0:rows_dev, :]
    input_grads = input_grads + tap_table[:, 1, None, :] * padded[:, 1 : 1 + rows_dev, :]
    input_grads = input_grads + tap_table[:, 2, None, :] * padded[:, 2 : 2 + rows_dev, :]
    input_grads = input_grads.astype(jnp.bfloat16)
    tap_terms = jnp.stack(
        [
            jnp.sum(grad_stack * extended[:, 2 - tap_lag : 2 - tap_lag + rows_dev, :], axis=1)
            for tap_lag in range(3)
        ],
        axis=1,
    )
    tap_grads = lax.psum(tap_terms, "seq") / math.sqrt(total_rows)
    positions = counting(rows_dev * lax.axis_size("seq"))
    cosine_part, sine_part = phases(positions, freq_index, fft_length, -1)
    filter_grad = lax.psum_scatter(
        (matmul(cosine_part, cross_real) - matmul(sine_part, cross_imag)) / fft_length,
        "seq",
        scatter_dimension=0,
        tiled=True,
    ) / math.sqrt(total_rows * 2 * half_group)
    passed_grads = passed_along(input_grads, "pipe", -1)
    return (layer_out[None], passed_grads[None], filter_grad[None], tap_grads[None])


def solution(mesh):
    in_specs = (
        P("pipe", "seq", None),
        P("pipe", "seq", None),
        P("pipe", "seq", None),
        P("pipe", "seq", None),
        P("pipe", "seq", None),
        P("pipe", None, None, None),
    )
    out_specs = (
        P("pipe", "seq", None),
        P("pipe", None, "seq", None),
        P("pipe", "seq", None),
        P("pipe", None, None, None),
    )
    return jax.shard_map(local, mesh=mesh, in_specs=in_specs, out_specs=out_specs, check_vma=False)
```

profile of v0, /device:TPU:1, one launch (start us, length us, event | category | flops | bytes accessed | tf_op | source)
XLA Modules:
  0.0 868.8 jit_solution(2596454109309922963)
XLA Ops:
  41.4 13.8 %all-to-all-done.4 = bf16[16,2,16384]{2,1,0:T(2,128)(2,1)S(1)} async-done(((bf16[16,2,16384]{2,1,0:T(2,128)(2,1)}), bf16[16,2,16384]{2,1,0:T(2,128)(2,1)S(1)}, u32[]{:S(2)}, u32[]{:S(2)}) %all-to-all-start.4) | async-done | bytes 1048608 | tf_op jit(solution)/shard_map/all_to_all | solution.py:163
  61.1 21.2 %reshape.367 = f32[16,8,512,2,4]{1,0,4,3,2:T(8,128)} reshape(f32[1,128,4096]{1,2,0:T(8,128)S(1)} %copy.196) | data formatting | bytes 4194304 | tf_op jit(solution)/shard_map/convert_element_type | solution.py:164
  82.3 22.1 %fusion.148 = (f32[16,8,512,1,4]{1,0,4,3,2:T(8,128)}, f32[16,8,512,1,4]{1,0,4,3,2:T(8,128)}) fusion(f32[16,8,512,2,4]{1,0,4,3,2:T(8,128)} %reshape.367), kind=kLoop, calls=%fused_computation.235 | loop fusion | bytes 4194304 | tf_op jit(solution)/shard_map/slice | solution.py:71
  104.4 9.8 %copy.199 = f32[1,16,8,2048]{3,2,1,0:T(8,128)S(1)} copy(f32[1,16,8,2048]{2,1,3,0:T(8,128)} %bitcast.255) | data formatting | bytes 2097152 | tf_op jit(solution)/shard_map/stack;reshape;squeeze | solution.py:69
  114.2 9.8 %copy.200 = f32[1,16,8,2048]{3,2,1,0:T(8,128)S(1)} copy(f32[1,16,8,2048]{2,1,3,0:T(8,128)} %bitcast.253) | data formatting | bytes 2097152 | tf_op jit(solution)/shard_map/stack;reshape;squeeze | solution.py:69
  141.5 11.4 %fusion.44 = f32[256,256]{1,0:T(8,128)S(1)} fusion(f32[1,2048,256]{2,1,0:T(8,128)} %all-gather.3.cloned.1.call-done, s32[256]{0:T(256)S(1)} %add_bitcast_fusion), kind=kOutput, calls=%fused_computation.80 | convolution fusion | flops 1617952768 | bytes 2360320 | tf_op jit(solution)/shard_map/dot_general | solution.py:22
  152.9 17.0 %fusion.46 = f32[256,256]{1,0:T(8,128)S(1)} fusion(f32[1,2048,256]{2,1,0:T(8,128)S(1)} %copy-done.37, s32[256]{0:T(256)S(1)} %add_bitcast_fusion), kind=kOutput, calls=%fused_computation.82 | convolution fusion | flops 1617952768 | bytes 2360320 | tf_op jit(solution)/shard_map/dot_general | solution.py:22
  173.4 14.6 %all-to-all-done.5 = f32[2,32,8,2048]{3,2,0,1:T(8,128)} async-done(((f32[2,32,8,2048]{3,2,0,1:T(8,128)}), f32[2,32,8,2048]{3,2,0,1:T(8,128)}, u32[]{:S(2)}, u32[]{:S(2)}) %all-to-all-start.5) | async-done | bytes 4194336 | tf_op jit(solution)/shard_map/all_to_all | solution.py:175
  188.0 8.9 %fusion.18 = f32[2,2,128,2048]{2,3,0,1:T(8,128)S(1)} fusion(f32[2,128,2,128]{3,2,1,0:T(2,128)S(1)} %reshape.359, f32[2,2,16,8,2048]{4,3,0,1,2:T(8,128)} %bitcast.42), kind=kOutput, calls=%fused_computation.38 | convolution fusion | flops 3221225472 | bytes 8650752 | tf_op jit(solution)/shard_map/xrzb,zkbw->xkrw/dot_general | solution.py:49
  220.8 46.7 %all-to-all-done.6 = f32[2,2,128,2048]{3,0,1,2:T(2,128)} async-done(((f32[2,2,128,2048]{3,0,1,2:T(2,128)}), f32[2,2,128,2048]{3,0,1,2:T(2,128)}, u32[]{:S(2)}, u32[]{:S(2)}) %all-to-all-start.6) | async-done | bytes 4194336 | tf_op jit(solution)/shard_map/all_to_all | solution.py:185
  286.7 9.4 %pad_maximum_fusion.1 = f32[16,8,512,2,4]{0,4,2,1,3:T(4,128)S(1)} fusion(f32[16,8,512,1,4]{0,4,2,1,3:T(4,128)} %bitcast.259, f32[16,8,512,1,4]{0,4,2,1,3:T(4,128)} %bitcast.257), kind=kLoop, calls=%fused_computation.1 | loop fusion | flops 524288 | bytes 4194304 | tf_op jit(solution)/shard_map/stack | solution.py:80
  296.2 16.2 %copy.215 = f32[16,8,512,2,4]{0,1,4,3,2:T(8,128)} copy(f32[16,8,512,2,4]{0,4,2,1,3:T(4,128)S(1)} %pad_maximum_fusion.1) | data formatting | bytes 4194304 | tf_op jit(solution)/shard_map/stack | solution.py:80
  312.4 9.6 %copy.216 = f32[16,8,4096]{2,1,0:T(8,128)S(1)} copy(f32[16,8,4096]{0,1,2:T(8,128)} %bitcast.251) | data formatting | bytes 4194304 | tf_op jit(solution)/shard_map/reshape | solution.py:81
  322.1 35.0 %all_to_all.102 = f32[16,8,4096]{2,1,0:T(8,128)S(1)} all-to-all(f32[16,8,4096]{2,1,0:T(8,128)S(1)} %copy.216), channel_id=1, replica_groups=mesh['seq'=16,'pipe'=8] {'seq'}, dimensions={0} | all-to-all | bytes 4194304 | tf_op jit(solution)/shard_map/all_to_all | solution.py:190
  364.8 8.4 reduce.1
  375.1 16.0 %all_to_all.103 = bf16[16,2,16384]{2,1,0:T(2,128)(2,1)S(1)} all-to-all(bf16[16,2,16384]{2,1,0:T(2,128)(2,1)} %reshape.382), channel_id=1, replica_groups=mesh['seq'=16,'pipe'=8] {'seq'}, dimensions={0} | all-to-all | bytes 2097152 | tf_op jit(solution)/shard_map/all_to_all | solution.py:163
  402.0 21.9 %reshape.366 = f32[16,8,512,2,4]{1,0,4,3,2:T(8,128)} reshape(f32[1,128,4096]{1,2,0:T(8,128)} %copy.171) | data formatting | bytes 4194304 | tf_op jit(solution)/shard_map/convert_element_type | solution.py:164
  423.9 22.0 %fusion.149 = (f32[16,8,512,1,4]{1,0,4,3,2:T(8,128)}, f32[16,8,512,1,4]{1,0,4,3,2:T(8,128)}) fusion(f32[16,8,512,2,4]{1,0,4,3,2:T(8,128)} %reshape.366), kind=kLoop, calls=%fused_computation.236 | loop fusion | bytes 4194304 | tf_op jit(solution)/shard_map/slice | solution.py:71
  445.8 9.8 %copy.174 = f32[1,16,8,2048]{3,2,1,0:T(8,128)S(1)} copy(f32[1,16,8,2048]{2,1,3,0:T(8,128)} %bitcast.256) | data formatting | bytes 2097152 | tf_op jit(solution)/shard_map/stack;reshape;squeeze | solution.py:69
  455.6 10.6 %copy.175 = f32[1,16,8,2048]{3,2,1,0:T(8,128)} copy(f32[1,16,8,2048]{2,1,3,0:T(8,128)} %bitcast.254) | data formatting | bytes 2097152 | tf_op jit(solution)/shard_map/stack;reshape;squeeze | solution.py:69
  476.5 47.8 %all_to_all.104 = f32[2,32,8,2048]{3,2,0,1:T(8,128)S(1)} all-to-all(f32[2,32,8,2048]{3,2,0,1:T(8,128)S(1)} %pad_maximum_fusion.4), channel_id=1, replica_groups=mesh['seq'=16,'pipe'=8] {'seq'}, dimensions={1} | all-to-all | bytes 8388608 | tf_op jit(solution)/shard_map/all_to_all | solution.py:175
  524.3 8.7 %fusion.15 = f32[2,2,128,2048]{2,3,0,1:T(8,128)} fusion(f32[2,128,2,128]{3,2,1,0:T(2,128)S(1)} %copy-done.11, f32[2,2,16,8,2048]{4,3,0,1,2:T(8,128)S(1)} %bitcast.263), kind=kOutput, calls=%fused_computation.37 | convolution fusion | flops 3221225472 | bytes 8650752 | tf_op jit(solution)/shard_map/xrzb,zkbw->xkrw/dot_general | solution.py:49
  553.6 47.2 %all_to_all.105 = f32[2,2,128,2048]{3,0,1,2:T(2,128)S(1)} all-to-all(f32[2,2,128,2048]{3,0,1,2:T(2,128)} %copy.187), channel_id=1, replica_groups=mesh['seq'=16,'pipe'=8] {'seq'}, dimensions={2} | all-to-all | bytes 8388608 | tf_op jit(solution)/shard_map/all_to_all | solution.py:185
  620.0 9.4 %pad_maximum_fusion = f32[16,8,512,2,4]{0,4,2,1,3:T(4,128)S(1)} fusion(f32[16,8,512,1,4]{0,4,2,1,3:T(4,128)} %bitcast.260, f32[16,8,512,1,4]{0,4,2,1,3:T(4,128)} %bitcast.258), kind=kLoop, calls=%fused_computation | loop fusion | flops 524288 | bytes 4194304 | tf_op jit(solution)/shard_map/stack | solution.py:80
  629.5 16.2 %copy.192 = f32[16,8,512,2,4]{0,1,4,3,2:T(8,128)} copy(f32[16,8,512,2,4]{0,4,2,1,3:T(4,128)S(1)} %pad_maximum_fusion) | data formatting | bytes 4194304 | tf_op jit(solution)/shard_map/stack | solution.py:80
  645.7 10.6 %copy.193 = f32[16,8,4096]{2,1,0:T(8,128)} copy(f32[16,8,4096]{0,1,2:T(8,128)} %bitcast.252) | data formatting | bytes 4194304 | tf_op jit(solution)/shard_map/reshape | solution.py:81
  666.9 9.6 %fusion.49 = f32[2048,256]{1,0:T(8,128)S(1)} fusion(f32[256,256]{1,0:T(8,128)S(1)} %bitcast.291, s32[256]{0:T(256)S(1)} %copy-done.36), kind=kOutput, calls=%fused_computation.87 | convolution fusion | flops 1617952768 | bytes 2360320 | tf_op jit(solution)/shard_map/dot_general | solution.py:22
  676.6 11.7 %fusion.23 = f32[2048,256]{1,0:T(8,128)} fusion(f32[2048,256]{1,0:T(8,128)S(1)} %fusion.49, f32[256,256]{1,0:T(8,128)S(1)} %bitcast.290, s32[256]{0:T(256)S(1)} %copy-done.36), kind=kOutput, calls=%fused_computation.48 | convolution fusion | flops 1619001344 | bytes 4457472 | tf_op jit(solution)/shard_map/dot_general | solution.py:22
  702.3 9.4 %multiply_reduce_fusion.2 = (f32[3,4096]{1,0:T(4,128)S(1)}, f32[3,4096]{1,0:T(4,128)S(1)}, f32[3,4096]{1,0:T(4,128)S(1)}, bf16[3,128,4096]{2,1,0:T(8,128)(2,1)}) fusion(f32[3,130,4096]{2,1,0:T(8,128)S(1)} %bitcast.250, f32[1,128,4096]{2,1,0:T(8,128)} %get-tuple-element.14, f32[1,128,4096]{2,1,0:T(8,128)S(1)} %get-tuple-element.13, ...), kind=kLoop, calls=%fused_computation.11 | loop fusion | flops 21983232 | bytes 41189376 | tf_op jit(solution)/shard_map/reduce_sum | solution.py:211
  711.6 11.9 %collective-permute-start.2 = (bf16[3,128,4096]{2,1,0:T(8,128)(2,1)}, bf16[3,128,4096]{2,1,0:T(8,128)(2,1)S(1)}, u32[]{:S(2)}, u32[]{:S(2)}) collective-permute-start(bf16[3,128,4096]{2,1,0:T(8,128)(2,1)} %get-tuple-element.19), channel_id=1, source_target_pairs={{1,0},{2,1},{3,2},{4,3},{5,4},{6,5},{7,6},{9,8},{10,9},{11,10},{12... | collective-permute-start | bytes 9437192 | tf_op jit(solution)/shard_map/ppermute | solution.py:14
  724.5 47.4 %reduce-scatter.2.cloned.1.call-done = f32[128,256]{1,0:T(8,128)} async-done(((f32[2048,256]{1,0:T(8,128)}), f32[128,256]{1,0:T(8,128)}) %reduce-scatter.2.cloned.1.call-update) | async-done | bytes 131088 | tf_op jit(solution)/shard_map/reduce_scatter | solution.py:219
  773.5 84.9 %all-reduce.2.cloned.1.call-done = f32[3,3,4096]{2,1,0:T(4,128)} async-done(((f32[3,3,4096]{2,1,0:T(4,128)}), f32[3,3,4096]{2,1,0:T(4,128)}) %all-reduce.2.cloned.1.call-update) | async-done | bytes 147472 | tf_op jit(solution)/shard_map/psum | solution.py:216
  (197 shorter events, 204.5 us)
Async XLA Ops:
  8.7 4.5 copy-start.24
  9.2 5.2 collective-permute-start
  32.8 22.4 %all-to-all-start.4 = ((bf16[16,2,16384]{2,1,0:T(2,128)(2,1)}), bf16[16,2,16384]{2,1,0:T(2,128)(2,1)S(1)}, u32[]{:S(2)}, u32[]{:S(2)}) async-start(bf16[16,2,16384]{2,1,0:T(2,128)(2,1)} %reshape.384), calls=%async_computation.4 | async-start | bytes 2097152 | tf_op jit(solution)/shard_map/all_to_all | solution.py:163
  40.3 101.1 %all-gather.3.cloned.1.call-start = ((), (), s32[]{:S(2)}) async-start(), calls=%async_computation.11 | async-start | bytes 2228224 | tf_op jit(solution)/shard_map/all_gather | solution.py:155
  41.3 84.1 %copy-start.22 = (f32[32,16]{1,0:T(8,128)}, f32[32,16]{1,0:T(8,128)S(1)}, u32[]{:S(2)}) copy-start(f32[32,16]{1,0:T(8,128)S(1)} %get-tuple-element.53) | copy-start | bytes 6148
  134.8 53.2 %all-to-all-start.5 = ((f32[2,32,8,2048]{3,2,0,1:T(8,128)}), f32[2,32,8,2048]{3,2,0,1:T(8,128)}, u32[]{:S(2)}, u32[]{:S(2)}) async-start(f32[2,32,8,2048]{3,2,0,1:T(8,128)} %pad_maximum_fusion.6), calls=%async_computation.5 | async-start | bytes 8388608 | tf_op jit(solution)/shard_map/all_to_all | solution.py:175
  140.5 47.5 %copy-start.10 = (f32[2,128,2,128]{3,2,1,0:T(2,128)}, f32[2,128,2,128]{3,2,1,0:T(2,128)S(1)}, u32[]{:S(2)}) copy-start(f32[2,128,2,128]{3,2,1,0:T(2,128)S(1)} %reshape.359) | copy-start | bytes 786436
  141.2 57.8 %copy-start.12 = (f32[2,128,2,128]{3,2,1,0:T(2,128)}, f32[2,128,2,128]{3,2,1,0:T(2,128)S(1)}, u32[]{:S(2)}) copy-start(f32[2,128,2,128]{3,2,1,0:T(2,128)S(1)} %reshape.360) | copy-start | bytes 786436
  141.3 28.6 %copy-start.31 = (s32[2048]{0:T(1024)}, s32[2048]{0:T(1024)S(1)}, u32[]{:S(2)}) copy-start(s32[2048]{0:T(1024)S(1)} %add_select_fusion.5) | copy-start | bytes 24580
  141.3 11.5 %copy-start.35 = (s32[256]{0:T(256)}, s32[256]{0:T(256)S(1)}, u32[]{:S(2)}) copy-start(s32[256]{0:T(256)S(1)} %add_bitcast_fusion) | copy-start | bytes 3076
  141.5 61.1 %copy-start.33 = (f32[2,128]{1,0:T(2,128)}, f32[2,128]{1,0:T(2,128)S(1)}, u32[]{:S(2)}) copy-start(f32[2,128]{1,0:T(2,128)S(1)} %get-tuple-element.47) | copy-start | bytes 3076
  141.5 11.4 %copy-start.37 = (f32[1,2048,256]{2,1,0:T(8,128)S(1)}, f32[1,2048,256]{2,1,0:T(8,128)}, u32[]{:S(2)}) copy-start(f32[1,2048,256]{2,1,0:T(8,128)} %all-gather.3.cloned.1.call-done) | copy-start | bytes 6291460
  188.0 8.9 %copy-start.1 = (f32[2,2,128,2048]{2,3,0,1:T(8,128)S(1)}, f32[2,2,128,2048]{2,3,0,1:T(8,128)}, u32[]{:S(2)}) copy-start(f32[2,2,128,2048]{2,3,0,1:T(8,128)} %fusion.61) | copy-start | bytes 12582916
  212.5 55.0 %all-to-all-start.6 = ((f32[2,2,128,2048]{3,0,1,2:T(2,128)}), f32[2,2,128,2048]{3,0,1,2:T(2,128)}, u32[]{:S(2)}, u32[]{:S(2)}) async-start(f32[2,2,128,2048]{3,0,1,2:T(2,128)} %copy.210), calls=%async_computation.6 | async-start | bytes 8388608 | tf_op jit(solution)/shard_map/all_to_all | solution.py:185
  220.8 54.4 %copy-start.25 = (f32[16,32]{1,0:T(8,128)}, f32[16,32]{1,0:T(8,128)S(1)}, u32[]{:S(2)}) copy-start(f32[16,32]{1,0:T(8,128)S(1)} %fusion.118) | copy-start | bytes 6148
  220.8 54.4 %copy-start.27 = (f32[16,32]{1,0:T(8,128)}, f32[16,32]{1,0:T(8,128)S(1)}, u32[]{:S(2)}) copy-start(f32[16,32]{1,0:T(8,128)S(1)} %get-tuple-element.58) | copy-start | bytes 6148
  220.8 54.4 %copy-start.29 = (f32[16,32]{1,0:T(8,128)}, f32[16,32]{1,0:T(8,128)S(1)}, u32[]{:S(2)}) copy-start(f32[16,32]{1,0:T(8,128)S(1)} %get-tuple-element.59) | copy-start | bytes 6148
  476.5 47.8 %copy-start.11 = (f32[2,128,2,128]{3,2,1,0:T(2,128)S(1)}, f32[2,128,2,128]{3,2,1,0:T(2,128)}, u32[]{:S(2)}) copy-start(f32[2,128,2,128]{3,2,1,0:T(2,128)} %copy-done.10) | copy-start | bytes 786436
  524.3 8.7 %copy-start.2 = (f32[2,2,128,2048]{2,3,0,1:T(8,128)S(1)}, f32[2,2,128,2048]{2,3,0,1:T(8,128)}, u32[]{:S(2)}) copy-start(f32[2,2,128,2048]{2,3,0,1:T(8,128)} %fusion.61) | copy-start | bytes 12582916
  524.3 8.7 %copy-start.4 = (f32[2,2,128,2048]{2,3,0,1:T(8,128)S(1)}, f32[2,2,128,2048]{2,3,0,1:T(8,128)}, u32[]{:S(2)}) copy-start(f32[2,2,128,2048]{2,3,0,1:T(8,128)} %copy-done.3) | copy-start | bytes 12582916
  533.0 5.4 copy-start.13
  538.4 5.1 copy-start.34
  656.3 4.8 copy-start.32
  656.3 32.0 %all-to-all-start.3 = ((f32[16,8,4096]{2,1,0:T(8,128)}), f32[16,8,4096]{2,1,0:T(8,128)}, u32[]{:S(2)}, u32[]{:S(2)}) async-start(f32[16,8,4096]{2,1,0:T(8,128)} %copy.193), calls=%async_computation.3 | async-start | bytes 4194304 | tf_op jit(solution)/shard_map/all_to_all | solution.py:190
  660.9 111.0 %reduce-scatter.2.cloned.1.call-start = ((), (), s32[]{:S(2)}) async-start(), calls=%async_computation.9 | async-start | bytes 2228224 | tf_op jit(solution)/shard_map/reduce_scatter | solution.py:219
  661.2 5.8 copy-start.36
  688.3 170.2 %all-reduce.2.cloned.1.call-start = ((), (), s32[]{:S(2)}) async-start(), calls=%async_computation.10 | async-start | bytes 393216 | tf_op jit(solution)/shard_map/psum | solution.py:216
  689.5 3.8 copy-start.6
  693.3 5.9 copy-start.7
  693.3 9.0 %slice-start = ((s8[6684672]{0:T(1024)(128)(4,1)}), s8[4194304]{0:T(1024)(128)(4,1)S(1)}, s32[]{:S(2)}) async-start(s8[6684672]{0:T(1024)(128)(4,1)} %bitcast.249), calls=%async_computation.12 | async-start | bytes 8388608
  694.0 5.1 collective-permute-start.1
  711.6 148.6 %collective-permute-start.2 = (bf16[3,128,4096]{2,1,0:T(8,128)(2,1)}, bf16[3,128,4096]{2,1,0:T(8,128)(2,1)S(1)}, u32[]{:S(2)}, u32[]{:S(2)}) collective-permute-start(bf16[3,128,4096]{2,1,0:T(8,128)(2,1)} %get-tuple-element.19), channel_id=1, source_target_pairs={{1,0},{2,1},{3,2},{4,3},{5,4},{6,5},{7,6},{9,8},{10,9},{11,10},{12... | collective-permute-start | bytes 9437192 | tf_op jit(solution)/shard_map/ppermute | solution.py:14
  (18 other events, 41.6 us)
Sparse Core Ops, SparseCore 0:
  43.3 47.9 all-gather.2
  688.4 83.4 reduce-scatter.1
  775.5 82.9 all-reduce.1
where the time goes:
time: 880 us; the launch traced here: 869 us
  local copies, waits for them, and re-layouts  267 us (30%)
  waiting for transfers between devices  212 us (24%)
  blocking collectives  146 us (17%)
  matrix products  96.2 us (11%)
  other arithmetic  88.4 us (10%)
  starting transfers between devices  43 us (5%)
  between operations  15.2 us (2%)
    psum x1, waiting for transfers between devices, local(): tap_grads = lax.psum(tap_terms, 'seq') / math.sqrt(total_rows)  84.9 us
    dot_general x8, matrix products, matmul(): jnp.dot(left, right, precision=exact_mode, preferred_element_type=jnp.flo...  60.9 us
    convert_element_type x4, local copies, waits for them, and re-layouts, forward(): packed = pack_pairs(arrived.astype(jnp.float32), pack_block)  47.8 us
    all_to_all x1, blocking collectives, forward(): lax.all_to_all(turned, 'seq', split_axis=1, concat_axis=2, tiled=True)  47.8 us
    reduce_scatter x1, waiting for transfers between devices, local(): lax.psum_scatter((matmul(cosine_part, cross_real) - matmul(sine_part, cro...  47.4 us
    all_to_all x1, blocking collectives, inverse(): lax.all_to_all(turned, 'seq', split_axis=2, concat_axis=1, tiled=True)  47.2 us
    all_to_all x1, waiting for transfers between devices, inverse(): lax.all_to_all(turned, 'seq', split_axis=2, concat_axis=1, tiled=True)  46.7 us
    slice x2, local copies, waits for them, and re-layouts, pack_pairs(): split_view[..., 0, :].reshape(lead_dims + (-1,))  44.1 us
  transfers between devices with their start and end apart: 10, of which 7 were waited for; matrix products, arithmetic and copies ran while one was open for 19% of the time, Pallas kernels for 0%

commit v1 on v0

v1 whole, which is shorter than its diff:
```python
import functools
import math

import jax
import jax.numpy as jnp
from jax import lax
from jax.experimental import pallas as pl
from jax.experimental.pallas import tpu as pltpu
from jax.sharding import PartitionSpec as P

f32 = jnp.float32
bf16 = jnp.bfloat16

N = 16
R = 128
C = 4096
Q = 4
CQ = C // Q
G = 16
OC = CQ // N
GQ = OC // G
T = N * R
W = 256
PARAMS = pltpu.CompilerParams(vmem_limit_bytes=56 * 2**20)


def rows_down(x, first):
    row = lax.broadcasted_iota(jnp.int32, x.shape, 0)
    return jnp.where(row == 0, first, pltpu.roll(x, 1, 0))


def rows_up(x, last):
    row = lax.broadcasted_iota(jnp.int32, x.shape, 0)
    return jnp.where(row == x.shape[0] - 1, last, pltpu.roll(x, x.shape[0] - 1, 0))


def short_filter(x, halo2, halo1, taps):
    back1 = rows_down(x, halo1)
    back2 = rows_down(back1, halo2)
    return taps[0] * x + taps[1] * back1 + taps[2] * back2


def features(lanes, in_refs, halo_ref, taps_ref):
    out = []
    for w in range(3):
        x = in_refs[w][:, lanes].astype(f32)
        taps = [taps_ref[3 * w + j : 3 * w + j + 1, lanes] for j in range(3)]
        out.append(
            short_filter(
                x, halo_ref[2 * w : 2 * w + 1, lanes], halo_ref[2 * w + 1 : 2 * w + 2, lanes], taps
            )
        )
    return out


def build_band(h, band_ref, base_ref, count):
    for r in range(8):
        base_ref[:, r, :] = h if r == 0 else pltpu.roll(h, r, 1)
    band_ref[:, :, 0:R] = jnp.zeros((count, R, R), bf16)

    def group(g, carry):
        base = base_ref[g]
        for m in range(R // 16):
            low = base if m == 0 else pltpu.roll(base, 16 * m, 1)
            high = pltpu.roll(base, 16 * m + 8, 1)
            both = jnp.concatenate([low, high], axis=0)
            row = lax.broadcasted_iota(jnp.int32, (16, R), 0) + 16 * m
            lane = lax.broadcasted_iota(jnp.int32, (16, R), 1)
            band_ref[g, 16 * m : 16 * m + 16, R : 2 * R] = jnp.where(
                lane >= row, both[:, :R], 0.0
            ).astype(bf16)
            band_ref[g, 16 * m : 16 * m + 16, 2 * R :] = both[:, R:].astype(bf16)
        return carry

    lax.fori_loop(0, count, group, 0)


def pair_lanes(x):
    v = x.reshape(N // 2, 2, G, R)
    return jnp.concatenate([v[:, 0], v[:, 1]], axis=-1).reshape(N // 2 * G, 2 * R)


def convolve(x, s, band):
    x2, s2 = pair_lanes(x), pair_lanes(s)
    zeros = jnp.zeros(((N // 2 - 1) * G, 2 * R), bf16)
    xp = jnp.concatenate([zeros, x2], axis=0)
    sp = jnp.concatenate([s2, zeros], axis=0)
    rows = N // 2 * G
    conv = back = None
    for d in range(N // 2):
        w = jnp.concatenate(
            [
                band[:, R + 2 * R * d : R + 2 * R * d + 2 * R],
                band[:, 2 * R * d : 2 * R * d + 2 * R],
            ],
            axis=0,
        )
        top = (N // 2 - 1 - d) * G
        c = jnp.dot(xp[top : top + rows], w, preferred_element_type=f32)
        b = lax.dot_general(
            sp[d * G : d * G + rows], w, (((1,), (1,)), ((), ())), preferred_element_type=f32
        )
        conv = c if conv is None else conv + c
        back = b if back is None else back + b
    return conv, back


def correlate(x, s, gram_ref):
    xt = x.reshape(N * G, R).astype(f32).T.astype(bf16)
    sp = jnp.concatenate([s.reshape(N * G, R), jnp.zeros((N * G, R), bf16)], axis=0)
    for d in range(N // 2):
        right = jnp.concatenate(
            [sp[2 * d * G : 2 * d * G + N * G], sp[(2 * d + 1) * G : (2 * d + 1) * G + N * G]],
            axis=1,
        )
        gram = jnp.dot(xt, right, preferred_element_type=f32)
        if d == 0:
            row = lax.broadcasted_iota(jnp.int32, gram.shape, 0)
            lane = lax.broadcasted_iota(jnp.int32, gram.shape, 1)
            gram = jnp.where(lane >= row, gram, 0.0)
        gram_ref[:, 2 * R * d : 2 * R * d + 2 * R] = gram
    total = gram_ref[0:8, :]
    for m in range(1, R // 8):
        total = total + pltpu.roll(gram_ref[8 * m : 8 * m + 8, :], T - 8 * m, 1)
    return total


def feature_kernel(q_ref, k_ref, v_ref, g_ref, halo_ref, taps_ref, out_ref):
    lanes = slice(None)
    query, keyed, valued = features(lanes, (q_ref, k_ref, v_ref), halo_ref, taps_ref)
    product = (keyed * valued).astype(bf16).astype(f32)
    scaled = (g_ref[...].astype(f32) * query).astype(bf16).astype(f32)
    for i in range(W // OC):
        out_ref[0, i, 0] = product.T[i * OC : (i + 1) * OC].astype(bf16)
        out_ref[0, i, 1] = scaled.T[i * OC : (i + 1) * OC].astype(bf16)


def conv_kernel(recv_ref, h_ref, ret_ref, fold_ref, band_ref, base_ref, gram_ref):
    build_band(h_ref[...], band_ref, base_ref, Q * GQ)

    def group(n, carry):
        q, i = n // GQ, n % GQ
        rows = pl.ds(pl.multiple_of(i * G, G), G)
        x = recv_ref[q, :, 0, rows, :]
        s = recv_ref[q, :, 1, rows, :]
        conv, back = convolve(x, s, band_ref.at[n])
        for w, value in ((0, conv), (1, back)):
            value = value.astype(bf16)
            for half in range(2):
                part = value[:, half * R : (half + 1) * R]
                for j in range(N // 2):
                    ret_ref[q, 2 * j + half, w, rows, :] = part[j * G : (j + 1) * G]
        fold_ref[n] = correlate(x, s, gram_ref)
        return carry

    lax.fori_loop(0, Q * GQ, group, 0)


def unfold(fold_ref):
    total = fold_ref[:, 0, :]
    for r in range(1, 8):
        total = total + pltpu.roll(fold_ref[:, r, :], T - r, 1)
    return total * (1.0 / math.sqrt(T * G))


def unfold_kernel(fold_ref, out_ref):
    out_ref[...] = unfold(fold_ref)


def grads_of(w, grad, conv, back, keyed, valued):
    return (grad * conv, back * valued, back * keyed)[w]


def finish_kernel(
    q_ref, k_ref, v_ref, g_ref, halo_ref, taps_ref, ret_ref, edge_ref, out_ref, grads_ref, tap_ref
):
    lanes = slice(None)
    query, keyed, valued = features(lanes, (q_ref, k_ref, v_ref), halo_ref, taps_ref)
    ret = ret_ref[0].astype(f32)
    conv = jnp.concatenate([ret[i, 0] for i in range(W // OC)], axis=0).T
    back = jnp.concatenate([ret[i, 1] for i in range(W // OC)], axis=0).T
    grad = g_ref[...].astype(f32)
    out_ref[...] = (query * conv).astype(bf16)
    raw = (q_ref, k_ref, v_ref)
    for w, g0 in enumerate((grad * conv, back * valued, back * keyed)):
        g1 = rows_up(g0, edge_ref[2 * w : 2 * w + 1, :])
        g2 = rows_up(g1, edge_ref[2 * w + 1 : 2 * w + 2, :])
        x = raw[w][...].astype(f32)
        total = None
        for j, g in enumerate((g0, g1, g2)):
            term = taps_ref[3 * w + j : 3 * w + j + 1, :] * g
            total = term if total is None else total + term
            tap_ref[3 * w + j : 3 * w + j + 1, :] = jnp.sum(g * x, axis=0, keepdims=True)
        grads_ref[w] = total.astype(bf16)


def edge_kernel(q_ref, k_ref, v_ref, g_ref, halo_ref, taps_ref, ret_ref, edge_ref):
    ret = ret_ref[0].astype(f32)
    conv = jnp.concatenate([ret[i, 0] for i in range(W // OC)], axis=0).T
    back = jnp.concatenate([ret[i, 1] for i in range(W // OC)], axis=0).T
    lanes = slice(None)
    query, keyed, valued = features(lanes, (q_ref, k_ref, v_ref), halo_ref, taps_ref)
    grad = g_ref[...].astype(f32)
    for w, g in enumerate((grad * conv, back * valued, back * keyed)):
        edge_ref[2 * w : 2 * w + 2, :] = g[0:2]
    edge_ref[6:8, :] = jnp.zeros((2, W), f32)


def passed(x, axis, by):
    count = lax.axis_size(axis)
    pairs = [(i, i + by) for i in range(count) if 0 <= i + by < count]
    return lax.ppermute(x, axis, pairs)


def exchange(x):
    return lax.all_to_all(x, "seq", split_axis=0, concat_axis=0, tiled=True)


def local(query_in, key_in, value_in, grad_out, long_filter, short_taps):
    raw = (query_in[0], key_in[0], value_in[0])
    grad = grad_out[0]
    taps = jnp.pad(short_taps[0].reshape(9, C), ((0, 7), (0, 0)))
    halo = passed(jnp.concatenate([x[R - 2 :] for x in raw], axis=0), "seq", 1)
    halo = jnp.pad(halo.astype(f32), ((0, 2), (0, 0)))
    turned = long_filter[0].T.reshape(Q, N, GQ, R).transpose(1, 0, 2, 3)
    h = exchange(turned).reshape(N, Q * GQ, R).transpose(1, 0, 2).reshape(Q * GQ, T)

    steps = C // W
    wide = lambda rows: pl.BlockSpec((rows, W), lambda n: (0, n))
    per = CQ // W
    owners = pl.BlockSpec(
        (1, W // OC, 2, OC, R), lambda n: (n // per, n % per, 0, 0, 0)
    )
    base_specs = [wide(R)] * 4 + [wide(8), wide(16)]
    sent = pl.pallas_call(
        feature_kernel,
        grid=(steps,),
        in_specs=base_specs,
        out_specs=owners,
        out_shape=jax.ShapeDtypeStruct((Q, N, 2, OC, R), bf16),
        compiler_params=PARAMS,
    )(*raw, grad, halo, taps)
    recv = lax.all_to_all(sent, "seq", split_axis=1, concat_axis=1, tiled=True)
    whole = pl.BlockSpec(memory_space=pltpu.VMEM)
    ret, fold = pl.pallas_call(
        conv_kernel,
        in_specs=[whole, whole],
        out_specs=[whole, whole],
        out_shape=[
            jax.ShapeDtypeStruct((Q, N, 2, OC, R), bf16),
            jax.ShapeDtypeStruct((Q * GQ, 8, T), f32),
        ],
        scratch_shapes=[
            pltpu.VMEM((Q * GQ, R, R + T), bf16),
            pltpu.VMEM((Q * GQ, 8, T), f32),
            pltpu.VMEM((R, T), f32),
        ],
        compiler_params=PARAMS,
    )(recv, h)
    ret = lax.all_to_all(ret, "seq", split_axis=1, concat_axis=1, tiled=True)
    unfolded = pl.pallas_call(
        unfold_kernel,
        in_specs=[whole],
        out_specs=whole,
        out_shape=jax.ShapeDtypeStruct((Q * GQ, T), f32),
        compiler_params=PARAMS,
    )(fold)
    pieces = exchange(unfolded.reshape(Q * GQ, N, R).transpose(1, 0, 2))
    filter_grad = pieces.reshape(N, Q, GQ, R).transpose(1, 0, 2, 3).reshape(C // G, R).T

    edge = pl.pallas_call(
        edge_kernel,
        grid=(steps,),
        in_specs=base_specs + [owners],
        out_specs=wide(8),
        out_shape=jax.ShapeDtypeStruct((8, C), f32),
        compiler_params=PARAMS,
    )(*raw, grad, halo, taps, ret)
    edge = passed(edge, "seq", -1)
    layer_out, input_grads, tap_sums = pl.pallas_call(
        finish_kernel,
        grid=(steps,),
        in_specs=base_specs + [owners, wide(8)],
        out_specs=[wide(R), pl.BlockSpec((3, R, W), lambda n: (0, 0, n)), wide(9)],
        out_shape=[
            jax.ShapeDtypeStruct((R, C), bf16),
            jax.ShapeDtypeStruct((3, R, C), bf16),
            jax.ShapeDtypeStruct((9, C), f32),
        ],
        compiler_params=PARAMS,
    )(*raw, grad, halo, taps, ret, edge)
    parts = exchange(tap_sums.reshape(9, N, C // N).transpose(1, 0, 2))
    owned = jnp.sum(parts, axis=0) * (1.0 / math.sqrt(T))
    tap_grads = exchange(jnp.broadcast_to(owned[None], (N, 9, C // N)))
    tap_grads = tap_grads.transpose(1, 0, 2).reshape(3, 3, C)
    passed_grads = passed(input_grads, "pipe", -1)
    return (layer_out[None], passed_grads[None], filter_grad[None], tap_grads[None])


def solution(mesh):
    in_specs = (
        P("pipe", "seq", None),
        P("pipe", "seq", None),
        P("pipe", "seq", None),
        P("pipe", "seq", None),
        P("pipe", "seq", None),
        P("pipe", None, None, None),
    )
    out_specs = (
        P("pipe", "seq", None),
        P("pipe", None, "seq", None),
        P("pipe", "seq", None),
        P("pipe", None, None, None),
    )
    return jax.shard_map(local, mesh=mesh, in_specs=in_specs, out_specs=out_specs, check_vma=False)
```

time: 880 us -> 204 us (0.23)
  local copies, waits for them, and re-layouts: 267 us -> 21.2 us
  waiting for transfers between devices: 212 us -> 49.6 us
  blocking collectives: 146 us -> 29.6 us
  matrix products: 96.2 us -> 0 us
  other arithmetic: 88.4 us -> 2.07 us
  Pallas kernels: 0 us -> 58.2 us
  between operations: 15.2 us -> 0.79 us
    all_to_all x4 -> x1, blocking collectives: 146 us -> 29.6 us  [local(): ret = lax.all_to_all(ret, 'seq', split_axis=1, concat_axis=1, tiled=True)]
    dot_general x14 -> x0, matrix products: 96.2 us -> none  [the longest x8 60.9 us: matmul(): jnp.dot(left, right, precision=exact_mode, preferred_element_type=jnp.flo...]
    another operation x12 -> x2, local copies, waits for them, and re-layouts: 87.2 us -> 0.89 us  [the longest x1 0.81 us: local(): tap_grads[None]]
    psum x1 -> x0, waiting for transfers between devices: 84.9 us -> none  [local(): tap_grads = lax.psum(tap_terms, 'seq') / math.sqrt(total_rows)]
    slice x14 -> x2, local copies, waits for them, and re-layouts: 65.9 us -> 1.77 us  [local(): halo = passed(jnp.concatenate([x[R - 2:] for x in raw], axis=0), 'seq', 1)]
    pallas_call x0 -> x5, Pallas kernels: none -> 58.2 us  [the longest x1 19.8 us: local(): pl.pallas_call(conv_kernel, in_specs=[whole, whole], out_specs=[whole, wh...]
    convert_element_type x6 -> x0, local copies, waits for them, and re-layouts: 53.9 us -> none  [the longest x4 47.8 us: forward(): packed = pack_pairs(arrived.astype(jnp.float32), pack_block)]
    reduce_scatter x1 -> x0, waiting for transfers between devices: 47.4 us -> none  [local(): lax.psum_scatter((matmul(cosine_part, cross_real) - matmul(sine_part, cro...]
  transfers between devices with their start and end apart: 10 -> 8, of which waited for: 7 -> 5; matrix products, arithmetic and copies ran while one was open for 19% -> 7% of each run, Pallas kernels for 0% -> 7%
where the time goes in v1:
time: 204 us; the launch traced here: 200 us
  Pallas kernels  58.2 us (29%)
  waiting for transfers between devices  49.6 us (24%)
  starting transfers between devices  38.5 us (19%)
  blocking collectives  29.6 us (15%)
  local copies, waits for them, and re-layouts  21.2 us (10%)
  other arithmetic  2.07 us (1%)
    all_to_all x1, blocking collectives, local(): ret = lax.all_to_all(ret, 'seq', split_axis=1, concat_axis=1, tiled=True)  29.6 us
    all_to_all x1, waiting for transfers between devices, local(): recv = lax.all_to_all(sent, 'seq', split_axis=1, concat_axis=1, tiled=True)  24.9 us
    all_to_all x4, waiting for transfers between devices, exchange(): return lax.all_to_all(x, 'seq', split_axis=0, concat_axis=0, tiled=True)  20.1 us
    pallas_call x1, Pallas kernels, local(): pl.pallas_call(conv_kernel, in_specs=[whole, whole], out_specs=[whole, wh...  19.8 us
    all_to_all x4, starting transfers between devices, exchange(): return lax.all_to_all(x, 'seq', split_axis=0, concat_axis=0, tiled=True)  18.7 us
    pallas_call x1, Pallas kernels, local(): pl.pallas_call(finish_kernel, grid=(steps,), in_specs=base_specs + [owner...  14.3 us
    ppermute x3, starting transfers between devices, passed(): return lax.ppermute(x, axis, pairs)  13.2 us
    pallas_call x1, Pallas kernels, local(): pl.pallas_call(feature_kernel, grid=(steps,), in_specs=base_specs, out_sp...  11.2 us
  transfers between devices with their start and end apart: 8, of which 5 were waited for; matrix products, arithmetic and copies ran while one was open for 7% of the time, Pallas kernels for 7%

profile of v1, /device:TPU:1, one launch (start us, length us, event | category | flops | bytes accessed | tf_op | source)
XLA Modules:
  0.0 200.0 jit_solution(4831233772735088922)
XLA Ops:
  0.6 0.9 slice_bitcast_fusion.2
  1.5 0.9 slice_bitcast_fusion
  2.5 4.0 %collective-permute-start = (bf16[6,4096]{1,0:T(8,128)(2,1)S(1)}, bf16[6,4096]{1,0:T(8,128)(2,1)S(1)}, u32[]{:S(2)}, u32[]{:S(2)}) collective-permute-start(bf16[6,4096]{1,0:T(8,128)(2,1)S(1)} %pad_maximum_fusion), channel_id=1, source_target_pairs={{0,8},{8,16},{16,24},{24,32},{32,40},{40,48},{48,56},{56,64},{64,7... | collective-permute-start | bytes 147464 | tf_op jit(solution)/shard_map/ppermute | solution.py:212
  6.5 1.0 copy.32
  8.2 6.5 %all-to-all-start.1 = ((f32[16,4,4,128]{3,2,1,0:T(4,128)}), f32[16,4,4,128]{3,2,1,0:T(4,128)S(1)}, u32[]{:S(2)}, u32[]{:S(2)}) async-start(f32[16,4,4,128]{3,2,1,0:T(4,128)} %copy.33), calls=%async_computation.1 | async-start | bytes 262144 | tf_op jit(solution)/shard_map/all_to_all | solution.py:216
  14.7 1.3 reduce
  17.5 11.2 %shard_map.93 = bf16[4,16,2,64,128]{4,3,2,1,0:T(8,128)(2,1)} custom-call(bf16[128,4096]{1,0:T(8,128)(2,1)} %bitcast.48, bf16[128,4096]{1,0:T(8,128)(2,1)} %bitcast.51, bf16[128,4096]{1,0:T(8,128)(2,1)} %bitcast.54, bf16[128,4096]{1,0:T(8,128)(2,1)} %bitcast.57, f32[8,4096]{1,0:T(8,128)} %pad_convert_fusion.halo_ref, f32[16,4096]{1,0:T(8,128)} %pad.12.taps_ref), custom_call_target="tpu_custom_call" | custom-call | tf_op jit(solution)/shard_map/pallas_call | solution.py:235
  28.7 3.2 %copy.31 = bf16[4,16,2,64,128]{4,3,2,0,1:T(8,128)(2,1)} copy(bf16[4,16,2,64,128]{4,3,2,1,0:T(8,128)(2,1)} %shard_map.93) | data formatting | bytes 4194304 | tf_op jit(solution)/shard_map/pallas_call | solution.py:235
  32.0 6.7 %all-to-all-start = ((bf16[4,16,2,64,128]{4,3,2,0,1:T(8,128)(2,1)}), bf16[4,16,2,64,128]{4,3,2,0,1:T(8,128)(2,1)S(1)}, u32[]{:S(2)}, u32[]{:S(2)}) async-start(bf16[4,16,2,64,128]{4,3,2,0,1:T(8,128)(2,1)} %copy.31), calls=%async_computation | async-start | bytes 4194304 | tf_op jit(solution)/shard_map/all_to_all | solution.py:243
  39.4 24.9 %all-to-all-done = bf16[4,16,2,64,128]{4,3,2,0,1:T(8,128)(2,1)S(1)} async-done(((bf16[4,16,2,64,128]{4,3,2,0,1:T(8,128)(2,1)}), bf16[4,16,2,64,128]{4,3,2,0,1:T(8,128)(2,1)S(1)}, u32[]{:S(2)}, u32[]{:S(2)}) %all-to-all-start) | async-done | bytes 2097184 | tf_op jit(solution)/shard_map/all_to_all | solution.py:243
  64.2 1.5 copy.35.recv_ref
  65.7 19.8 %shard_map.94 = (bf16[4,16,2,64,128]{4,3,2,1,0:T(8,128)(2,1)}, f32[16,8,2048]{2,1,0:T(8,128)}) custom-call(bf16[4,16,2,64,128]{4,3,2,1,0:T(8,128)(2,1)} %copy.35.recv_ref, f32[16,2048]{1,0:T(8,128)} %bitcast.64), custom_call_target="tpu_custom_call" | custom-call | tf_op jit(solution)/shard_map/pallas_call | solution.py:245
  85.5 1.8 copy.36
  87.3 29.6 %all_to_all.30 = bf16[4,16,2,64,128]{4,3,2,0,1:T(8,128)(2,1)S(1)} all-to-all(bf16[4,16,2,64,128]{4,3,2,0,1:T(8,128)(2,1)S(1)} %copy.36), channel_id=1, replica_groups=mesh['seq'=16,'pipe'=8] {'seq'}, dimensions={1} | all-to-all | bytes 4194304 | tf_op jit(solution)/shard_map/all_to_all | solution.py:260
  116.9 1.5 copy.38.ret_ref
  118.4 10.5 %shard_map.95 = f32[8,4096]{1,0:T(8,128)} custom-call(bf16[128,4096]{1,0:T(8,128)(2,1)} %bitcast.49, bf16[128,4096]{1,0:T(8,128)(2,1)} %bitcast.52, bf16[128,4096]{1,0:T(8,128)(2,1)} %bitcast.55, bf16[128,4096]{1,0:T(8,128)(2,1)} %bitcast.58, f32[8,4096]{1,0:T(8,128)} %pad_convert_fusion.halo_ref, f32[16,4096]{1,0:T(8,128)} %pad.12.taps_ref, ...), custom_call_target="tpu_custom_call" | custom-call | tf_op jit(solution)/shard_map/pallas_call | solution.py:271
  129.0 1.3 collective-permute-start.1
  130.2 4.6 %collective-permute-done.1.edge_ref = f32[8,4096]{1,0:T(8,128)S(1)} collective-permute-done((f32[8,4096]{1,0:T(8,128)}, f32[8,4096]{1,0:T(8,128)S(1)}, u32[]{:S(2)}, u32[]{:S(2)}) %collective-permute-start.1) | collective-permute-done | bytes 131104 | tf_op jit(solution)/shard_map/ppermute | solution.py:212
  135.5 14.3 %shard_map.96 = (bf16[128,4096]{1,0:T(8,128)(2,1)}, bf16[3,128,4096]{2,1,0:T(8,128)(2,1)}, f32[9,4096]{1,0:T(8,128)}) custom-call(bf16[128,4096]{1,0:T(8,128)(2,1)} %bitcast.50, bf16[128,4096]{1,0:T(8,128)(2,1)} %bitcast.53, bf16[128,4096]{1,0:T(8,128)(2,1)} %bitcast.56, bf16[128,4096]{1,0:T(8,128)(2,1)} %bitcast.59, f32[8,4096]{1,0:T(8,128)} %pad_convert_fusion.halo_ref, ...), custom_call_target="tpu_custom_call" | custom-call | tf_op jit(solution)/shard_map/pallas_call | solution.py:280
  149.9 7.9 %collective-permute-start.2 = (bf16[3,128,4096]{2,1,0:T(8,128)(2,1)}, bf16[3,128,4096]{2,1,0:T(8,128)(2,1)S(1)}, u32[]{:S(2)}, u32[]{:S(2)}) collective-permute-start(bf16[3,128,4096]{2,1,0:T(8,128)(2,1)} %get-tuple-element.11), channel_id=1, source_target_pairs={{1,0},{2,1},{3,2},{4,3},{5,4},{6,5},{7,6},{9,8},{10,9},{11,10},{12... | collective-permute-start | bytes 9437192 | tf_op jit(solution)/shard_map/ppermute | solution.py:212
  157.8 2.3 %shard_map.97 = f32[16,2048]{1,0:T(8,128)} custom-call(f32[16,8,2048]{2,1,0:T(8,128)} %get-tuple-element.12.fold_ref), custom_call_target="tpu_custom_call" | custom-call | tf_op jit(solution)/shard_map/pallas_call | solution.py:261
  160.0 1.0 copy.49
  161.1 0.8 copy.53
  161.9 4.8 %all-to-all-start.4 = ((f32[16,9,256]{2,1,0:T(8,128)}), f32[16,9,256]{2,1,0:T(8,128)S(1)}, u32[]{:S(2)}, u32[]{:S(2)}) async-start(f32[16,9,256]{2,1,0:T(8,128)} %bitcast.62), calls=%async_computation.4 | async-start | bytes 524288 | tf_op jit(solution)/shard_map/all_to_all | solution.py:216
  166.7 1.6 bitcast_bitcast_fusion
  168.3 6.9 %all-to-all-done.4 = f32[16,9,256]{2,1,0:T(8,128)S(1)} async-done(((f32[16,9,256]{2,1,0:T(8,128)}), f32[16,9,256]{2,1,0:T(8,128)S(1)}, u32[]{:S(2)}, u32[]{:S(2)}) %all-to-all-start.4) | async-done | bytes 147488 | tf_op jit(solution)/shard_map/all_to_all | solution.py:216
  175.2 3.8 %all-to-all-start.3 = ((f32[16,16,128]{2,1,0:T(8,128)}), f32[16,16,128]{2,1,0:T(8,128)S(1)}, u32[]{:S(2)}, u32[]{:S(2)}) async-start(f32[16,16,128]{2,1,0:T(8,128)} %bitcast_bitcast_fusion), calls=%async_computation.3 | async-start | bytes 262144 | tf_op jit(solution)/shard_map/all_to_all | solution.py:216
  179.1 6.8 %all-to-all-done.3 = f32[16,16,128]{2,1,0:T(8,128)S(1)} async-done(((f32[16,16,128]{2,1,0:T(8,128)}), f32[16,16,128]{2,1,0:T(8,128)S(1)}, u32[]{:S(2)}, u32[]{:S(2)}) %all-to-all-start.3) | async-done | bytes 131104 | tf_op jit(solution)/shard_map/all_to_all | solution.py:216
  186.6 3.5 %all-to-all-start.5 = ((f32[16,9,256]{2,1,0:T(8,128)}), f32[16,9,256]{2,1,0:T(8,128)S(1)}, u32[]{:S(2)}, u32[]{:S(2)}) async-start(f32[16,9,256]{2,1,0:T(8,128)} %broadcast_in_dim.18), calls=%async_computation.5 | async-start | bytes 524288 | tf_op jit(solution)/shard_map/all_to_all | solution.py:216
  191.0 6.4 %all-to-all-done.5 = f32[16,9,256]{2,1,0:T(8,128)S(1)} async-done(((f32[16,9,256]{2,1,0:T(8,128)}), f32[16,9,256]{2,1,0:T(8,128)S(1)}, u32[]{:S(2)}, u32[]{:S(2)}) %all-to-all-start.5) | async-done | bytes 147488 | tf_op jit(solution)/shard_map/all_to_all | solution.py:216
  197.5 0.8 broadcast_in_dim_reshape.4
  198.3 1.7 copy.56
  (20 shorter events, 5.3 us)
Async XLA Ops:
  2.5 14.3 %collective-permute-start = (bf16[6,4096]{1,0:T(8,128)(2,1)S(1)}, bf16[6,4096]{1,0:T(8,128)(2,1)S(1)}, u32[]{:S(2)}, u32[]{:S(2)}) collective-permute-start(bf16[6,4096]{1,0:T(8,128)(2,1)S(1)} %pad_maximum_fusion), channel_id=1, source_target_pairs={{0,8},{8,16},{16,24},{24,32},{32,40},{40,48},{48,56},{56,64},{64,7... | collective-permute-start | bytes 147464 | tf_op jit(solution)/shard_map/ppermute | solution.py:212
  8.2 23.8 %all-to-all-start.1 = ((f32[16,4,4,128]{3,2,1,0:T(4,128)}), f32[16,4,4,128]{3,2,1,0:T(4,128)S(1)}, u32[]{:S(2)}, u32[]{:S(2)}) async-start(f32[16,4,4,128]{3,2,1,0:T(4,128)} %copy.33), calls=%async_computation.1 | async-start | bytes 262144 | tf_op jit(solution)/shard_map/all_to_all | solution.py:216
  32.0 32.3 %all-to-all-start = ((bf16[4,16,2,64,128]{4,3,2,0,1:T(8,128)(2,1)}), bf16[4,16,2,64,128]{4,3,2,0,1:T(8,128)(2,1)S(1)}, u32[]{:S(2)}, u32[]{:S(2)}) async-start(bf16[4,16,2,64,128]{4,3,2,0,1:T(8,128)(2,1)} %copy.31), calls=%async_computation | async-start | bytes 4194304 | tf_op jit(solution)/shard_map/all_to_all | solution.py:243
  129.0 5.9 %collective-permute-start.1 = (f32[8,4096]{1,0:T(8,128)}, f32[8,4096]{1,0:T(8,128)S(1)}, u32[]{:S(2)}, u32[]{:S(2)}) collective-permute-start(f32[8,4096]{1,0:T(8,128)} %shard_map.95), channel_id=1, source_target_pairs={{8,0},{16,8},{24,16},{32,24},{40,32},{48,40},{56,48},{64,56},{72,6... | collective-permute-start | bytes 393224 | tf_op jit(solution)/shard_map/ppermute | solution.py:212
  134.9 0.7 copy-start
  149.9 48.5 %collective-permute-start.2 = (bf16[3,128,4096]{2,1,0:T(8,128)(2,1)}, bf16[3,128,4096]{2,1,0:T(8,128)(2,1)S(1)}, u32[]{:S(2)}, u32[]{:S(2)}) collective-permute-start(bf16[3,128,4096]{2,1,0:T(8,128)(2,1)} %get-tuple-element.11), channel_id=1, source_target_pairs={{1,0},{2,1},{3,2},{4,3},{5,4},{6,5},{7,6},{9,8},{10,9},{11,10},{12... | collective-permute-start | bytes 9437192 | tf_op jit(solution)/shard_map/ppermute | solution.py:212
  161.9 13.3 %all-to-all-start.4 = ((f32[16,9,256]{2,1,0:T(8,128)}), f32[16,9,256]{2,1,0:T(8,128)S(1)}, u32[]{:S(2)}, u32[]{:S(2)}) async-start(f32[16,9,256]{2,1,0:T(8,128)} %bitcast.62), calls=%async_computation.4 | async-start | bytes 524288 | tf_op jit(solution)/shard_map/all_to_all | solution.py:216
  175.2 10.7 %all-to-all-start.3 = ((f32[16,16,128]{2,1,0:T(8,128)}), f32[16,16,128]{2,1,0:T(8,128)S(1)}, u32[]{:S(2)}, u32[]{:S(2)}) async-start(f32[16,16,128]{2,1,0:T(8,128)} %bitcast_bitcast_fusion), calls=%async_computation.3 | async-start | bytes 262144 | tf_op jit(solution)/shard_map/all_to_all | solution.py:216
  186.6 10.8 %all-to-all-start.5 = ((f32[16,9,256]{2,1,0:T(8,128)}), f32[16,9,256]{2,1,0:T(8,128)S(1)}, u32[]{:S(2)}, u32[]{:S(2)}) async-start(f32[16,9,256]{2,1,0:T(8,128)} %broadcast_in_dim.18), calls=%async_computation.5 | async-start | bytes 524288 | tf_op jit(solution)/shard_map/all_to_all | solution.py:216

commit v2 on v1

v2 whole, which is shorter than its diff:
```python
import functools
import math

import jax
import jax.numpy as jnp
from jax import lax
from jax.experimental import pallas as pl
from jax.experimental.pallas import tpu as pltpu
from jax.sharding import PartitionSpec as P

f32 = jnp.float32
bf16 = jnp.bfloat16

N = 16
R = 128
C = 4096
Q = 4
CQ = C // Q
G = 16
OC = CQ // N
GQ = OC // G
T = N * R
W = 256
B = CQ // W


def rows_down(x, first):
    row = lax.broadcasted_iota(jnp.int32, x.shape, 0)
    return jnp.where(row == 0, first, pltpu.roll(x, 1, 0))


def rows_up(x, last):
    row = lax.broadcasted_iota(jnp.int32, x.shape, 0)
    return jnp.where(row == x.shape[0] - 1, last, pltpu.roll(x, x.shape[0] - 1, 0))


def short_filter(x, halo2, halo1, taps):
    back1 = rows_down(x, halo1)
    back2 = rows_down(back1, halo2)
    return taps[0] * x + taps[1] * back1 + taps[2] * back2


def features(lanes, in_refs, halo_ref, taps_ref):
    out = []
    for w in range(3):
        x = in_refs[w][:, lanes].astype(f32)
        taps = [taps_ref[w, j : j + 1, lanes] for j in range(3)]
        out.append(
            short_filter(
                x, halo_ref[2 * w : 2 * w + 1, lanes], halo_ref[2 * w + 1 : 2 * w + 2, lanes], taps
            )
        )
    return out


def build_band(h, band_ref, base_ref, count):
    for r in range(8):
        base_ref[:, r, :] = h if r == 0 else pltpu.roll(h, r, 1)
    band_ref[:, :, 0:R] = jnp.zeros((count, R, R), bf16)

    def group(g, carry):
        base = base_ref[g]
        for m in range(R // 16):
            low = base if m == 0 else pltpu.roll(base, 16 * m, 1)
            high = pltpu.roll(base, 16 * m + 8, 1)
            both = jnp.concatenate([low, high], axis=0)
            row = lax.broadcasted_iota(jnp.int32, (16, R), 0) + 16 * m
            lane = lax.broadcasted_iota(jnp.int32, (16, R), 1)
            band_ref[g, 16 * m : 16 * m + 16, R : 2 * R] = jnp.where(
                lane >= row, both[:, :R], 0.0
            ).astype(bf16)
            band_ref[g, 16 * m : 16 * m + 16, 2 * R :] = both[:, R:].astype(bf16)
        return carry

    lax.fori_loop(0, count, group, 0)


def pair_lanes(x):
    v = x.reshape(N // 2, 2, G, R)
    return jnp.concatenate([v[:, 0], v[:, 1]], axis=-1).reshape(N // 2 * G, 2 * R)


def convolve(x, s, band):
    x2, s2 = pair_lanes(x), pair_lanes(s)
    zeros = jnp.zeros(((N // 2 - 1) * G, 2 * R), bf16)
    xp = jnp.concatenate([zeros, x2], axis=0)
    sp = jnp.concatenate([s2, zeros], axis=0)
    rows = N // 2 * G
    conv = back = None
    for d in range(N // 2):
        w = jnp.concatenate(
            [
                band[:, R + 2 * R * d : R + 2 * R * d + 2 * R],
                band[:, 2 * R * d : 2 * R * d + 2 * R],
            ],
            axis=0,
        )
        top = (N // 2 - 1 - d) * G
        c = jnp.dot(xp[top : top + rows], w, preferred_element_type=f32)
        b = lax.dot_general(
            sp[d * G : d * G + rows], w, (((1,), (1,)), ((), ())), preferred_element_type=f32
        )
        conv = c if conv is None else conv + c
        back = b if back is None else back + b
    return conv, back


def correlate(x, s, gram_ref):
    xt = x.reshape(N * G, R).astype(f32).T.astype(bf16)
    sp = jnp.concatenate([s.reshape(N * G, R), jnp.zeros((N * G, R), bf16)], axis=0)
    for d in range(N // 2):
        right = jnp.concatenate(
            [sp[2 * d * G : 2 * d * G + N * G], sp[(2 * d + 1) * G : (2 * d + 1) * G + N * G]],
            axis=1,
        )
        gram = jnp.dot(xt, right, preferred_element_type=f32)
        if d == 0:
            row = lax.broadcasted_iota(jnp.int32, gram.shape, 0)
            lane = lax.broadcasted_iota(jnp.int32, gram.shape, 1)
            gram = jnp.where(lane >= row, gram, 0.0)
        gram_ref[:, 2 * R * d : 2 * R * d + 2 * R] = gram
    total = gram_ref[0:8, :]
    for m in range(1, R // 8):
        total = total + pltpu.roll(gram_ref[8 * m : 8 * m + 8, :], T - 8 * m, 1)
    return total


def block(n, size):
    return pl.ds(pl.multiple_of(n * size, size), size)


def whole_kernel(
    q_ref, k_ref, v_ref, g_ref, filter_ref, taps_ref,
    out_ref, passed_ref, fgrad_ref, tap_ref,
    feat, send, recv, ret_send, ret_recv, band, base, gram, fold, slabs, zeros,
    halo_out, halo_in, edge_out, edge_in, filt_out, filt_in, fg_out, fg_in, fg_rows,
    tap_out, tap_in, sum_out, sum_in,
    s_halo, r_halo, s_filt, r_filt, s_fwd, r_fwd, s_ret, r_ret, s_edge, r_edge,
    s_pipe, r_pipe, s_fg, r_fg, s_tap, r_tap, s_sum, r_sum, s_zero,
):
    me = lax.axis_index("seq")
    pipe = lax.axis_index("pipe")
    sections = lax.axis_size("pipe")
    raw = (q_ref, k_ref, v_ref)

    def peer_of(s):
        return lax.rem(me + s, N)

    def each_peer(fn):
        def step(s, carry):
            fn(peer_of(s))
            return carry

        lax.fori_loop(1, N, step, 0)

    def remote(src, dst, s_sem, r_sem, where):
        return pltpu.make_async_remote_copy(
            src_ref=src, dst_ref=dst, send_sem=s_sem, recv_sem=r_sem,
            device_id=where, device_id_type=pl.DeviceIdType.MESH,
        )

    def spread(src, dst, s_sem, r_sem):
        def start(k):
            remote(src.at[k], dst.at[me], s_sem.at[k], r_sem.at[me], {"seq": k}).start()

        def wait_recv(k):
            remote(src.at[k], dst.at[k], s_sem.at[k], r_sem.at[k], {"seq": k}).wait_recv()

        def wait_send(k):
            remote(src.at[k], dst.at[k], s_sem.at[k], r_sem.at[k], {"seq": k}).wait_send()

        return start, wait_recv, wait_send

    barrier = pltpu.get_barrier_semaphore()

    def greet(k):
        pl.semaphore_signal(
            barrier, inc=1, device_id={"seq": k}, device_id_type=pl.DeviceIdType.MESH
        )

    each_peer(greet)
    for by in (1, sections - 1):
        pl.semaphore_signal(
            barrier, inc=1, device_id={"pipe": lax.rem(pipe + by, sections)},
            device_id_type=pl.DeviceIdType.MESH,
        )

    for w in range(3):
        last = raw[w][R - 16 : R, :].astype(f32)
        halo_out[2 * w : 2 * w + 2, :] = last[14:16]
    halo_out[6:8, :] = jnp.zeros((2, C), f32)
    turned = filter_ref[...].T
    for k in range(N):
        for q in range(Q):
            first = q * N * GQ + k * GQ
            filt_out[k, q * GQ : (q + 1) * GQ, :] = turned[first : first + GQ]
    filt_in[me] = filt_out[me]

    pl.semaphore_wait(barrier, N + 1)

    def halo_copy():
        return remote(halo_out, halo_in, s_halo, r_halo, {"seq": jnp.minimum(me + 1, N - 1)})

    @pl.when(me < N - 1)
    def _():
        halo_copy().start()

    filt = spread(filt_out, filt_in, s_filt, r_filt)
    each_peer(filt[0])

    @pl.when(me == 0)
    def _():
        halo_in[...] = jnp.zeros_like(halo_in)

    @pl.when(me > 0)
    def _():
        halo_copy().wait_recv()

    fwd = [spread(send.at[q], recv.at[q], s_fwd.at[q], r_fwd.at[q]) for q in range(Q)]
    ret = [spread(ret_send.at[q], ret_recv.at[q], s_ret.at[q], r_ret.at[q]) for q in range(Q)]

    def feature_phase(q):
        def step(b, carry):
            n = q * B + b
            lanes = block(n, W)
            query, keyed, valued = features(lanes, raw, halo_in, taps_ref)
            feat[0, :, lanes] = query
            feat[1, :, lanes] = keyed
            feat[2, :, lanes] = valued
            product = (keyed * valued).astype(bf16).astype(f32).T
            scaled = (g_ref[:, lanes].astype(f32) * query).astype(bf16).astype(f32).T
            for i in range(W // OC):
                send[q, b * (W // OC) + i, 0] = product[i * OC : (i + 1) * OC].astype(bf16)
                send[q, b * (W // OC) + i, 1] = scaled[i * OC : (i + 1) * OC].astype(bf16)
            return carry

        lax.fori_loop(0, B, step, 0)
        each_peer(fwd[q][0])
        recv[q, me] = send[q, me]

    def conv_phase(q):
        each_peer(fwd[q][1])

        def group(i, carry):
            rows = block(i, G)
            conv, back = convolve(
                recv[q, :, 0, rows, :], recv[q, :, 1, rows, :], band.at[q * GQ + i]
            )
            for w, value in ((0, conv), (1, back)):
                value = value.astype(bf16)
                for half in range(2):
                    part = value[:, half * R : (half + 1) * R]
                    for j in range(N // 2):
                        ret_send[q, 2 * j + half, w, rows, :] = part[j * G : (j + 1) * G]
            return carry

        lax.fori_loop(0, GQ, group, 0)
        each_peer(ret[q][0])
        ret_recv[q, me] = ret_send[q, me]

    def corr_phase(q):
        def group(i, carry):
            rows = block(i, G)
            fold[q * GQ + i] = correlate(
                recv[q, :, 0, rows, :], recv[q, :, 1, rows, :], gram
            )
            return carry

        lax.fori_loop(0, GQ, group, 0)

    def edge_copy(q):
        return remote(
            edge_out.at[q], edge_in.at[q], s_edge.at[q], r_edge.at[q],
            {"seq": jnp.maximum(me - 1, 0)},
        )

    def grad_phase(q):
        each_peer(ret[q][1])

        def step(b, carry):
            lanes = block(q * B + b, W)
            owners = W // OC
            got = [
                jnp.concatenate(
                    [ret_recv[q, b * owners + i, w].astype(f32) for i in range(owners)], axis=0
                ).T
                for w in range(2)
            ]
            conv, back = got
            grad = g_ref[:, lanes].astype(f32)
            out_ref[:, lanes] = (feat[0, :, lanes] * conv).astype(bf16)
            grads = (grad * conv, back * feat[2, :, lanes], back * feat[1, :, lanes])
            for w in range(3):
                feat[w, :, lanes] = grads[w]
                edge_out[q, 2 * w : 2 * w + 2, block(b, W)] = grads[w][0:2]
            edge_out[q, 6:8, block(b, W)] = jnp.zeros((2, W), f32)
            return carry

        lax.fori_loop(0, B, step, 0)

        @pl.when(me > 0)
        def _():
            edge_copy(q).start()

        @pl.when(me == N - 1)
        def _():
            edge_in[q] = jnp.zeros((8, CQ), f32)

    tap_start, tap_wait_recv, tap_wait_send = spread(tap_out, tap_in, s_tap, r_tap)

    def pipe_copy(q):
        return remote(
            slabs.at[q], passed_ref.at[:, :, q * CQ : (q + 1) * CQ], s_pipe.at[q], r_pipe.at[q],
            {"pipe": jnp.maximum(pipe - 1, 0)},
        )

    def input_phase(q):
        @pl.when(me < N - 1)
        def _():
            edge_copy(q).wait_recv()

        def step(b, carry):
            n = q * B + b
            lanes = block(n, W)
            near = block(b, W)
            for w in range(3):
                g0 = feat[w, :, lanes]
                g1 = rows_up(g0, edge_in[q, 2 * w : 2 * w + 1, near])
                g2 = rows_up(g1, edge_in[q, 2 * w + 1 : 2 * w + 2, near])
                x = raw[w][:, lanes].astype(f32)
                total = None
                for j, g in enumerate((g0, g1, g2)):
                    term = taps_ref[w, j : j + 1, lanes] * g
                    total = term if total is None else total + term
                    tap_out[n, 3 * w + j : 3 * w + j + 1, :] = jnp.sum(g * x, axis=0, keepdims=True)
                slabs[q, w, :, near] = total.astype(bf16)

            @pl.when(n == me)
            def _():
                tap_in[n] = tap_out[n]

            @pl.when(n != me)
            def _():
                tap_start(n)

            return carry

        lax.fori_loop(0, B, step, 0)

        @pl.when(pipe > 0)
        def _():
            pipe_copy(q).start()

    def filter_phase():
        each_peer(filt[1])
        h = jnp.concatenate([filt_in[j] for j in range(N)], axis=1)
        build_band(h, band, base, Q * GQ)

    fg_start, fg_wait_recv, fg_wait_send = spread(fg_out, fg_in, s_fg, r_fg)

    def unfold_phase():
        total = fold[:, 0, :]
        for r in range(1, 8):
            total = total + pltpu.roll(fold[:, r, :], T - r, 1)
        total = total * (1.0 / math.sqrt(T * G))
        for k in range(N):
            fg_out[k] = total[:, k * R : (k + 1) * R]
        fg_in[me] = fg_out[me]
        each_peer(fg_start)

    def fgrad_phase():
        each_peer(fg_wait_recv)
        for k in range(N):
            for q in range(Q):
                first = q * N * GQ + k * GQ
                fg_rows[first : first + GQ, :] = fg_in[k, q * GQ : (q + 1) * GQ, :]
        fgrad_ref[...] = fg_rows[...].T

    def zero_copy():
        return pltpu.make_async_copy(zeros, passed_ref, s_zero)

    @pl.when(pipe == sections - 1)
    def _():
        zeros[...] = jnp.zeros_like(zeros)
        zero_copy().start()

    feature_phase(0)
    feature_phase(1)
    filter_phase()
    feature_phase(2)
    feature_phase(3)
    conv_phase(0)
    conv_phase(1)
    corr_phase(0)
    conv_phase(2)
    corr_phase(1)
    grad_phase(0)
    conv_phase(3)
    corr_phase(2)
    input_phase(0)
    grad_phase(1)
    corr_phase(3)
    unfold_phase()
    input_phase(1)
    grad_phase(2)
    input_phase(2)
    grad_phase(3)
    input_phase(3)

    each_peer(tap_wait_recv)
    owned = tap_in[0]
    for k in range(1, N):
        owned = owned + tap_in[k]
    sum_out[...] = owned * (1.0 / math.sqrt(T))
    sum_in[me] = sum_out[...]

    def sum_copy(k, slot):
        return remote(sum_out, sum_in.at[slot], s_sum.at[k], r_sum.at[slot], {"seq": k})

    each_peer(lambda k: sum_copy(k, me).start())
    fgrad_phase()
    each_peer(lambda k: sum_copy(k, k).wait_recv())
    for k in range(N):
        for w in range(3):
            tap_ref[w, :, k * W : (k + 1) * W] = sum_in[k, 3 * w : 3 * w + 3, :]

    @pl.when(me < N - 1)
    def _():
        halo_copy().wait_send()

    each_peer(filt[2])
    for q in range(Q):
        each_peer(fwd[q][2])
        each_peer(ret[q][2])
    each_peer(fg_wait_send)
    each_peer(tap_wait_send)
    each_peer(lambda k: sum_copy(k, k).wait_send())

    @pl.when(me > 0)
    def _():
        for q in range(Q):
            edge_copy(q).wait_send()

    @pl.when(pipe > 0)
    def _():
        for q in range(Q):
            pipe_copy(q).wait_send()

    @pl.when(pipe < sections - 1)
    def _():
        for q in range(Q):
            pipe_copy(q).wait_recv()

    @pl.when(pipe == sections - 1)
    def _():
        zero_copy().wait()


def local(query_in, key_in, value_in, grad_out, long_filter, short_taps):
    vmem = pl.BlockSpec(memory_space=pltpu.VMEM)
    hbm = pl.BlockSpec(memory_space=pl.ANY)
    dma = pltpu.SemaphoreType.DMA
    layer_out, passed_grads, filter_grad, tap_grads = pl.pallas_call(
        whole_kernel,
        in_specs=[vmem] * 6,
        out_specs=[vmem, hbm, vmem, vmem],
        out_shape=[
            jax.ShapeDtypeStruct((R, C), bf16),
            jax.ShapeDtypeStruct((3, R, C), bf16),
            jax.ShapeDtypeStruct((R, C // G), f32),
            jax.ShapeDtypeStruct((3, 3, C), f32),
        ],
        scratch_shapes=[
            pltpu.VMEM((3, R, C), f32),
            pltpu.VMEM((Q, N, 2, OC, R), bf16),
            pltpu.VMEM((Q, N, 2, OC, R), bf16),
            pltpu.VMEM((Q, N, 2, OC, R), bf16),
            pltpu.VMEM((Q, N, 2, OC, R), bf16),
            pltpu.VMEM((Q * GQ, R, R + T), bf16),
            pltpu.VMEM((Q * GQ, 8, T), f32),
            pltpu.VMEM((R, T), f32),
            pltpu.VMEM((Q * GQ, 8, T), f32),
            pltpu.VMEM((Q, 3, R, CQ), bf16),
            pltpu.VMEM((3, R, C), bf16),
            pltpu.VMEM((8, C), f32),
            pltpu.VMEM((8, C), f32),
            pltpu.VMEM((Q, 8, CQ), f32),
            pltpu.VMEM((Q, 8, CQ), f32),
            pltpu.VMEM((N, Q * GQ, R), f32),
            pltpu.VMEM((N, Q * GQ, R), f32),
            pltpu.VMEM((N, Q * GQ, R), f32),
            pltpu.VMEM((N, Q * GQ, R), f32),
            pltpu.VMEM((C // G, R), f32),
            pltpu.VMEM((N, 9, W), f32),
            pltpu.VMEM((N, 9, W), f32),
            pltpu.VMEM((9, W), f32),
            pltpu.VMEM((N, 9, W), f32),
            dma, dma,
            dma((N,)), dma((N,)),
            dma((Q, N)), dma((Q, N)),
            dma((Q, N)), dma((Q, N)),
            dma((Q,)), dma((Q,)),
            dma((Q,)), dma((Q,)),
            dma((N,)), dma((N,)),
            dma((N,)), dma((N,)),
            dma((N,)), dma((N,)),
            dma,
        ],
        compiler_params=pltpu.CompilerParams(
            collective_id=0, has_side_effects=True, vmem_limit_bytes=60 * 2**20
        ),
    )(query_in[0], key_in[0], value_in[0], grad_out[0], long_filter[0], short_taps[0])
    return (layer_out[None], passed_grads[None], filter_grad[None], tap_grads[None])


def solution(mesh):
    in_specs = (
        P("pipe", "seq", None),
        P("pipe", "seq", None),
        P("pipe", "seq", None),
        P("pipe", "seq", None),
        P("pipe", "seq", None),
        P("pipe", None, None, None),
    )
    out_specs = (
        P("pipe", "seq", None),
        P("pipe", None, "seq", None),
        P("pipe", "seq", None),
        P("pipe", None, None, None),
    )
    return jax.shard_map(local, mesh=mesh, in_specs=in_specs, out_specs=out_specs, check_vma=False)
```

time: 204 us -> 120 us (0.59); the launches traced: 200 us -> 119 us
  Pallas kernels: 58.2 us -> 108 us
  waiting for transfers between devices: 49.6 us -> 0 us
  starting transfers between devices: 38.5 us -> 0 us
  blocking collectives: 29.6 us -> 0 us
  local copies, waits for them, and re-layouts: 21.2 us -> 10.3 us
  other arithmetic: 2.07 us -> 0 us
    pallas_call x5 -> x1, Pallas kernels: 58.2 us -> 108 us  [local(): pl.pallas_call(whole_kernel, in_specs=[vmem] * 6, out_specs=[vmem, hbm, v...]
    all_to_all x5 -> x0, waiting for transfers between devices: 44.9 us -> none  [the longest x1 24.9 us: local(): recv = lax.all_to_all(sent, 'seq', split_axis=1, concat_axis=1, tiled=True)]
    all_to_all x1 -> x0, blocking collectives: 29.6 us -> none  [local(): ret = lax.all_to_all(ret, 'seq', split_axis=1, concat_axis=1, tiled=True)]
    all_to_all x5 -> x0, starting transfers between devices: 25.3 us -> none  [the longest x4 18.7 us: exchange(): return lax.all_to_all(x, 'seq', split_axis=0, concat_axis=0, tiled=True)]
    ppermute x3 -> x0, starting transfers between devices: 13.2 us -> none  [passed(): return lax.ppermute(x, axis, pairs)]
    pallas_call x2 -> x0, local copies, waits for them, and re-layouts: 4.99 us -> none  [the longest x1 3.23 us: local(): pl.pallas_call(feature_kernel, grid=(steps,), in_specs=base_specs, out_sp...]
    ppermute x3 -> x0, waiting for transfers between devices: 4.63 us -> none  [passed(): return lax.ppermute(x, axis, pairs)]
    unnamed x7, local copies, waits for them, and re-layouts: 5.8 us -> 10.3 us
  transfers between devices with their start and end apart: 8 -> 0, of which waited for: 5 -> 0; matrix products, arithmetic and copies ran while one was open for 7% -> 0% of each run, Pallas kernels for 7% -> 0%
where the time goes in v2:
time: 120 us; the launch traced here: 119 us
  Pallas kernels  108 us (90%)
  local copies, waits for them, and re-layouts  10.3 us (9%)
    pallas_call x1, Pallas kernels, local(): pl.pallas_call(whole_kernel, in_specs=[vmem] * 6, out_specs=[vmem, hbm, v...  108 us
    unnamed x7, local copies, waits for them, and re-layouts  10.3 us

profile of v2, /device:TPU:1, one launch (start us, length us, event | category | flops | bytes accessed | tf_op | source)
XLA Modules:
  0.0 119.4 jit_solution(2372838430077627991)
XLA Ops:
  0.6 1.7 %copy.13 = f32[1,3,3,4096]{3,2,0,1:T(4,128)} copy(f32[1,3,3,4096]{3,0,2,1:T(1,128)} %param.11) | data formatting | bytes 294912
  2.3 108.5 %shard_map.93 = (bf16[128,4096]{1,0:T(8,128)(2,1)}, bf16[3,128,4096]{2,1,0:T(8,128)(2,1)}, f32[128,256]{1,0:T(8,128)}, f32[3,3,4096]{2,1,0:T(4,128)}) custom-call(bf16[128,4096]{1,0:T(8,128)(2,1)} %bitcast.13, bf16[128,4096]{1,0:T(8,128)(2,1)} %bitcast.14, bf16[128,4096]{1,0:T(8,128)(2,1)} %bitcast.15, bf16[128,4096]{1,0:T(8,128)(2,1)} %bitcast.16, ...), custom_call_target="tpu_custom_call" | custom-call | tf_op jit(solution)/shard_map/pallas_call | solution.py:463
  110.8 1.7 %copy.10 = f32[1,3,3,4096]{3,0,2,1:T(1,128)} copy(f32[1,3,3,4096]{3,2,1,0:T(4,128)} %bitcast.19) | data formatting | bytes 294912
  112.5 2.3 %copy.17 = bf16[1,128,4096]{2,1,0:T(8,128)(2,1)} copy(bf16[1,128,4096]{2,1,0:T(8,128)(2,1)} %bitcast.17) | data formatting | bytes 2097152
  114.8 0.0 copy-start
  114.8 3.9 %copy.18 = bf16[1,3,128,4096]{3,2,1,0:T(8,128)(2,1)} copy(bf16[1,3,128,4096]{3,2,1,0:T(8,128)(2,1)} %bitcast.12) | data formatting | bytes 6291456
  118.8 0.0 copy-done
  118.8 0.7 copy.19
Async XLA Ops:
  114.8 3.9 %copy-start = (f32[128,256]{1,0:T(8,128)S(1)}, f32[128,256]{1,0:T(8,128)}, u32[]{:S(2)}) copy-start(f32[128,256]{1,0:T(8,128)} %get-tuple-element.10) | copy-start | bytes 393220

commit v3 on v2

--- a/solution.py
+++ b/solution.py
@@ -14,7 +14,7 @@
 N = 16
 R = 128
 C = 4096
-Q = 4
+Q = 8
 CQ = C // Q
 G = 16
 OC = CQ // N
@@ -22,6 +22,10 @@
 T = N * R
 W = 256
 B = CQ // W
+HALVES = 2
+TW = C // N // HALVES
+AHEAD = 2
+LAG = 1
 
 
 def rows_down(x, first):
@@ -44,7 +48,7 @@
     out = []
     for w in range(3):
         x = in_refs[w][:, lanes].astype(f32)
-        taps = [taps_ref[w, j : j + 1, lanes] for j in range(3)]
+        taps = [taps_ref[3 * w + j, :, lanes] for j in range(3)]
         out.append(
             short_filter(
                 x, halo_ref[2 * w : 2 * w + 1, lanes], halo_ref[2 * w + 1 : 2 * w + 2, lanes], taps
@@ -53,26 +57,22 @@
     return out
 
 
-def build_band(h, band_ref, base_ref, count):
+def build_base(h, base_ref):
     for r in range(8):
         base_ref[:, r, :] = h if r == 0 else pltpu.roll(h, r, 1)
-    band_ref[:, :, 0:R] = jnp.zeros((count, R, R), bf16)
-
-    def group(g, carry):
-        base = base_ref[g]
-        for m in range(R // 16):
-            low = base if m == 0 else pltpu.roll(base, 16 * m, 1)
-            high = pltpu.roll(base, 16 * m + 8, 1)
-            both = jnp.concatenate([low, high], axis=0)
-            row = lax.broadcasted_iota(jnp.int32, (16, R), 0) + 16 * m
-            lane = lax.broadcasted_iota(jnp.int32, (16, R), 1)
-            band_ref[g, 16 * m : 16 * m + 16, R : 2 * R] = jnp.where(
-                lane >= row, both[:, :R], 0.0
-            ).astype(bf16)
-            band_ref[g, 16 * m : 16 * m + 16, 2 * R :] = both[:, R:].astype(bf16)
-        return carry
-
-    lax.fori_loop(0, count, group, 0)
+
+
+def build_band(base, band_ref):
+    band_ref[:, 0:R] = jnp.zeros((R, R), bf16)
+    for m in range(R // 16):
+        low = base if m == 0 else pltpu.roll(base, 16 * m, 1)
+        high = pltpu.roll(base, 16 * m + 8, 1)
+        both = jnp.concatenate([low, high], axis=0)
+        row = lax.broadcasted_iota(jnp.int32, (16, R), 0) + 16 * m
+        lane = lax.broadcasted_iota(jnp.int32, (16, R), 1)
+        rows = slice(16 * m, 16 * m + 16)
+        band_ref[rows, R : 2 * R] = jnp.where(lane >= row, both[:, :R], 0.0).astype(bf16)
+        band_ref[rows, 2 * R :] = both[:, R:].astype(bf16)
 
 
 def pair_lanes(x):
@@ -130,18 +130,25 @@
 
 
 def whole_kernel(
-    q_ref, k_ref, v_ref, g_ref, filter_ref, taps_ref,
-    out_ref, passed_ref, fgrad_ref, tap_ref,
-    feat, send, recv, ret_send, ret_recv, band, base, gram, fold, slabs, zeros,
-    halo_out, halo_in, edge_out, edge_in, filt_out, filt_in, fg_out, fg_in, fg_rows,
+    q_hbm, k_hbm, v_hbm, g_hbm, filter_ref, taps_ref,
+    out_hbm, passed_ref, fgrad_ref, tap_ref,
+    inputs, out_ref, feat, send, recv, ret_send, ret_recv, band, base, gram, fold, slabs, zeros,
+    halo_out, halo_in, edge_out, edge_in, filt_pack, filt_out, filt_in, fg_out, fg_in, fg_rows,
     tap_out, tap_in, sum_out, sum_in,
     s_halo, r_halo, s_filt, r_filt, s_fwd, r_fwd, s_ret, r_ret, s_edge, r_edge,
-    s_pipe, r_pipe, s_fg, r_fg, s_tap, r_tap, s_sum, r_sum, s_zero,
+    s_pipe, r_pipe, s_fg, r_fg, s_tap, r_tap, s_sum, r_sum, s_zero, s_in, s_out,
 ):
     me = lax.axis_index("seq")
     pipe = lax.axis_index("pipe")
     sections = lax.axis_size("pipe")
-    raw = (q_ref, k_ref, v_ref)
+    raw = tuple(inputs.at[w] for w in range(3))
+    g_ref = inputs.at[3]
+
+    def load(w):
+        return pltpu.make_async_copy((q_hbm, k_hbm, v_hbm, g_hbm)[w], inputs.at[w], s_in.at[w])
+
+    for w in range(4):
+        load(w).start()
 
     def peer_of(s):
         return lax.rem(me + s, N)
@@ -185,6 +192,8 @@
             device_id_type=pl.DeviceIdType.MESH,
         )
 
+    for w in range(4):
+        load(w).wait()
     for w in range(3):
         last = raw[w][R - 16 : R, :].astype(f32)
         halo_out[2 * w : 2 * w + 2, :] = last[14:16]
@@ -193,17 +202,23 @@
     for k in range(N):
         for q in range(Q):
             first = q * N * GQ + k * GQ
-            filt_out[k, q * GQ : (q + 1) * GQ, :] = turned[first : first + GQ]
+            filt_pack[k, q * GQ : (q + 1) * GQ, :] = turned[first : first + GQ]
+    filt_out[...] = filt_pack[...].astype(bf16)
     filt_in[me] = filt_out[me]
 
     pl.semaphore_wait(barrier, N + 1)
 
-    def halo_copy():
-        return remote(halo_out, halo_in, s_halo, r_halo, {"seq": jnp.minimum(me + 1, N - 1)})
+    def halo_copy(q):
+        lanes = block(q, CQ)
+        return remote(
+            halo_out.at[:, lanes], halo_in.at[:, lanes], s_halo.at[q], r_halo.at[q],
+            {"seq": jnp.minimum(me + 1, N - 1)},
+        )
 
     @pl.when(me < N - 1)
     def _():
-        halo_copy().start()
+        for q in range(Q):
+            halo_copy(q).start()
 
     filt = spread(filt_out, filt_in, s_filt, r_filt)
     each_peer(filt[0])
@@ -212,14 +227,17 @@
     def _():
         halo_in[...] = jnp.zeros_like(halo_in)
 
-    @pl.when(me > 0)
-    def _():
-        halo_copy().wait_recv()
-
-    fwd = [spread(send.at[q], recv.at[q], s_fwd.at[q], r_fwd.at[q]) for q in range(Q)]
-    ret = [spread(ret_send.at[q], ret_recv.at[q], s_ret.at[q], r_ret.at[q]) for q in range(Q)]
+    def fwd(q):
+        return spread(send.at[q], recv.at[q], s_fwd.at[q], r_fwd.at[q])
+
+    def ret(q):
+        return spread(ret_send.at[q], ret_recv.at[q], s_ret.at[q], r_ret.at[q])
 
     def feature_phase(q):
+        @pl.when(me > 0)
+        def _():
+            halo_copy(q).wait_recv()
+
         def step(b, carry):
             n = q * B + b
             lanes = block(n, W)
@@ -235,11 +253,18 @@
             return carry
 
         lax.fori_loop(0, B, step, 0)
-        each_peer(fwd[q][0])
+        each_peer(fwd(q)[0])
         recv[q, me] = send[q, me]
 
+    def band_phase(q):
+        def group(i, carry):
+            build_band(base[q * GQ + i], band.at[q * GQ + i])
+            return carry
+
+        lax.fori_loop(0, GQ, group, 0)
+
     def conv_phase(q):
-        each_peer(fwd[q][1])
+        each_peer(fwd(q)[1])
 
         def group(i, carry):
             rows = block(i, G)
@@ -255,7 +280,7 @@
             return carry
 
         lax.fori_loop(0, GQ, group, 0)
-        each_peer(ret[q][0])
+        each_peer(ret(q)[0])
         ret_recv[q, me] = ret_send[q, me]
 
     def corr_phase(q):
@@ -274,8 +299,12 @@
             {"seq": jnp.maximum(me - 1, 0)},
         )
 
+    def out_copy(q):
+        lanes = block(q, CQ)
+        return pltpu.make_async_copy(out_ref.at[:, lanes], out_hbm.at[:, lanes], s_out.at[q])
+
     def grad_phase(q):
-        each_peer(ret[q][1])
+        each_peer(ret(q)[1])
 
         def step(b, carry):
             lanes = block(q * B + b, W)
@@ -298,6 +327,8 @@
 
         lax.fori_loop(0, B, step, 0)
 
+        out_copy(q).start()
+
         @pl.when(me > 0)
         def _():
             edge_copy(q).start()
@@ -306,11 +337,12 @@
         def _():
             edge_in[q] = jnp.zeros((8, CQ), f32)
 
-    tap_start, tap_wait_recv, tap_wait_send = spread(tap_out, tap_in, s_tap, r_tap)
+    def tap(half):
+        return spread(tap_out.at[half], tap_in.at[half], s_tap.at[half], r_tap.at[half])
 
     def pipe_copy(q):
         return remote(
-            slabs.at[q], passed_ref.at[:, :, q * CQ : (q + 1) * CQ], s_pipe.at[q], r_pipe.at[q],
+            slabs.at[q], passed_ref.at[:, :, block(q, CQ)], s_pipe.at[q], r_pipe.at[q],
             {"pipe": jnp.maximum(pipe - 1, 0)},
         )
 
@@ -330,31 +362,33 @@
                 x = raw[w][:, lanes].astype(f32)
                 total = None
                 for j, g in enumerate((g0, g1, g2)):
-                    term = taps_ref[w, j : j + 1, lanes] * g
+                    term = taps_ref[3 * w + j, :, lanes] * g
                     total = term if total is None else total + term
-                    tap_out[n, 3 * w + j : 3 * w + j + 1, :] = jnp.sum(g * x, axis=0, keepdims=True)
+                    part = jnp.sum(g * x, axis=0, keepdims=True)
+                    for i in range(W // TW):
+                        owner = lax.rem(n * (W // TW) + i, N)
+                        half = lax.div(n * (W // TW), N)
+                        tap_out[half, owner, 3 * w + j : 3 * w + j + 1, :] = part[:, i * TW : (i + 1) * TW]
                 slabs[q, w, :, near] = total.astype(bf16)
-
-            @pl.when(n == me)
+            return carry
+
+        lax.fori_loop(0, B, step, 0)
+
+        @pl.when(pipe > 0)
+        def _():
+            pipe_copy(q).start()
+
+        for half in range(HALVES):
+
+            @pl.when(q == (half + 1) * (Q // HALVES) - 1)
             def _():
-                tap_in[n] = tap_out[n]
-
-            @pl.when(n != me)
-            def _():
-                tap_start(n)
-
-            return carry
-
-        lax.fori_loop(0, B, step, 0)
-
-        @pl.when(pipe > 0)
-        def _():
-            pipe_copy(q).start()
+                each_peer(tap(half)[0])
+                tap_in[half, me] = tap_out[half, me]
 
     def filter_phase():
         each_peer(filt[1])
-        h = jnp.concatenate([filt_in[j] for j in range(N)], axis=1)
-        build_band(h, band, base, Q * GQ)
+        h = jnp.concatenate([filt_in[j].astype(f32) for j in range(N)], axis=1)
+        build_base(h, base)
 
     fg_start, fg_wait_recv, fg_wait_send = spread(fg_out, fg_in, s_fg, r_fg)
 
@@ -379,62 +413,99 @@
     def zero_copy():
         return pltpu.make_async_copy(zeros, passed_ref, s_zero)
 
-    @pl.when(pipe == sections - 1)
-    def _():
-        zeros[...] = jnp.zeros_like(zeros)
-        zero_copy().start()
-
-    feature_phase(0)
-    feature_phase(1)
+    def sum_copy(half, k, slot):
+        return remote(
+            sum_out.at[half], sum_in.at[half, slot], s_sum.at[half, k], r_sum.at[half, slot], {"seq": k}
+        )
+
+    def sum_phase(half):
+        each_peer(tap(half)[1])
+        owned = tap_in[half, 0]
+        for k in range(1, N):
+            owned = owned + tap_in[half, k]
+        sum_out[half] = owned * (1.0 / math.sqrt(T))
+        sum_in[half, me] = sum_out[half]
+        each_peer(lambda k: sum_copy(half, k, me).start())
+
+    for q in range(AHEAD):
+        feature_phase(q)
+    def zero_phase():
+        @pl.when(pipe == sections - 1)
+        def _():
+            zeros[...] = jnp.zeros_like(zeros)
+            zero_copy().start()
+
     filter_phase()
-    feature_phase(2)
-    feature_phase(3)
-    conv_phase(0)
-    conv_phase(1)
-    corr_phase(0)
-    conv_phase(2)
-    corr_phase(1)
-    grad_phase(0)
-    conv_phase(3)
-    corr_phase(2)
-    input_phase(0)
-    grad_phase(1)
-    corr_phase(3)
-    unfold_phase()
-    input_phase(1)
-    grad_phase(2)
-    input_phase(2)
-    grad_phase(3)
-    input_phase(3)
-
-    each_peer(tap_wait_recv)
-    owned = tap_in[0]
-    for k in range(1, N):
-        owned = owned + tap_in[k]
-    sum_out[...] = owned * (1.0 / math.sqrt(T))
-    sum_in[me] = sum_out[...]
-
-    def sum_copy(k, slot):
-        return remote(sum_out, sum_in.at[slot], s_sum.at[k], r_sum.at[slot], {"seq": k})
-
-    each_peer(lambda k: sum_copy(k, me).start())
+    band_phase(0)
+
+    def step(t, carry):
+        @pl.when(t < Q)
+        def _():
+            conv_phase(t)
+
+        @pl.when(t + AHEAD < Q)
+        def _():
+            feature_phase(t + AHEAD)
+
+        @pl.when((t >= LAG) & (t < Q + LAG))
+        def _():
+            grad_phase(t - LAG)
+
+        @pl.when(t + 1 < Q)
+        def _():
+            band_phase(t + 1)
+
+        @pl.when(t < Q)
+        def _():
+            corr_phase(t)
+
+        @pl.when(t == Q - 1)
+        def _():
+            unfold_phase()
+
+        @pl.when(t == 0)
+        def _():
+            zero_phase()
+
+        @pl.when(t >= LAG + 1)
+        def _():
+            input_phase(t - LAG - 1)
+
+        @pl.when(t == Q // HALVES + LAG + 1)
+        def _():
+            sum_phase(0)
+
+        return carry
+
+    lax.fori_loop(0, Q + LAG + 1, step, 0)
+
+    sum_phase(1)
     fgrad_phase()
-    each_peer(lambda k: sum_copy(k, k).wait_recv())
-    for k in range(N):
-        for w in range(3):
-            tap_ref[w, :, k * W : (k + 1) * W] = sum_in[k, 3 * w : 3 * w + 3, :]
+    for half in range(HALVES):
+        each_peer(lambda k: sum_copy(half, k, k).wait_recv())
+        for k in range(N):
+            first = half * (C // HALVES) + k * TW
+            for r in range(9):
+                tap_ref[r, :, first : first + TW] = sum_in[half, k, r : r + 1, :]
 
     @pl.when(me < N - 1)
     def _():
-        halo_copy().wait_send()
+        for q in range(Q):
+            halo_copy(q).wait_send()
 
     each_peer(filt[2])
-    for q in range(Q):
-        each_peer(fwd[q][2])
-        each_peer(ret[q][2])
+
+    def sent(q, carry):
+        each_peer(fwd(q)[2])
+        each_peer(ret(q)[2])
+        out_copy(q).wait()
+        return carry
+
+    lax.fori_loop(0, Q, sent, 0)
     each_peer(fg_wait_send)
-    each_peer(tap_wait_send)
-    each_peer(lambda k: sum_copy(k, k).wait_send())
+    for half in range(HALVES):
+        each_peer(tap(half)[2])
+        each_peer(lambda k: sum_copy(half, k, k).wait_send())
 
     @pl.when(me > 0)
     def _():
@@ -454,6 +525,13 @@
     @pl.when(pipe == sections - 1)
     def _():
         zero_copy().wait()
+
+
+def copy_kernel(out_in, passed_in, fgrad_in, tap_in, out, passed, fgrad, tap):
+    out[...] = out_in[...]
+    passed[...] = passed_in[...]
+    fgrad[...] = fgrad_in[...]
+    tap[...] = tap_in[...]
 
 
 def local(query_in, key_in, value_in, grad_out, long_filter, short_taps):
@@ -462,15 +540,17 @@
     dma = pltpu.SemaphoreType.DMA
     layer_out, passed_grads, filter_grad, tap_grads = pl.pallas_call(
         whole_kernel,
-        in_specs=[vmem] * 6,
-        out_specs=[vmem, hbm, vmem, vmem],
+        in_specs=[hbm] * 4 + [vmem] * 2,
+        out_specs=[hbm, hbm, vmem, vmem],
         out_shape=[
             jax.ShapeDtypeStruct((R, C), bf16),
             jax.ShapeDtypeStruct((3, R, C), bf16),
             jax.ShapeDtypeStruct((R, C // G), f32),
-            jax.ShapeDtypeStruct((3, 3, C), f32),
+            jax.ShapeDtypeStruct((9, 1, C), f32),
         ],
         scratch_shapes=[
+            pltpu.VMEM((4, R, C), bf16),
+            pltpu.VMEM((R, C), bf16),
             pltpu.VMEM((3, R, C), f32),
             pltpu.VMEM((Q, N, 2, OC, R), bf16),
             pltpu.VMEM((Q, N, 2, OC, R), bf16),
@@ -487,30 +567,53 @@
             pltpu.VMEM((Q, 8, CQ), f32),
             pltpu.VMEM((Q, 8, CQ), f32),
             pltpu.VMEM((N, Q * GQ, R), f32),
-            pltpu.VMEM((N, Q * GQ, R), f32),
+            pltpu.VMEM((N, Q * GQ, R), bf16),
+            pltpu.VMEM((N, Q * GQ, R), bf16),
             pltpu.VMEM((N, Q * GQ, R), f32),
             pltpu.VMEM((N, Q * GQ, R), f32),
             pltpu.VMEM((C // G, R), f32),
-            pltpu.VMEM((N, 9, W), f32),
-            pltpu.VMEM((N, 9, W), f32),
-            pltpu.VMEM((9, W), f32),
-            pltpu.VMEM((N, 9, W), f32),
-            dma, dma,
+            pltpu.VMEM((HALVES, N, 9, TW), f32),
+            pltpu.VMEM((HALVES, N, 9, TW), f32),
+            pltpu.VMEM((HALVES, 9, TW), f32),
+            pltpu.VMEM((HALVES, N, 9, TW), f32),
+            dma((Q,)), dma((Q,)),
             dma((N,)), dma((N,)),
             dma((Q, N)), dma((Q, N)),
             dma((Q, N)), dma((Q, N)),
             dma((Q,)), dma((Q,)),
             dma((Q,)), dma((Q,)),
             dma((N,)), dma((N,)),
-            dma((N,)), dma((N,)),
-            dma((N,)), dma((N,)),
+            dma((HALVES, N)), dma((HALVES, N)),
+            dma((HALVES, N)), dma((HALVES, N)),
             dma,
+            dma((4,)),
+            dma((Q,)),
         ],
         compiler_params=pltpu.CompilerParams(
             collective_id=0, has_side_effects=True, vmem_limit_bytes=60 * 2**20
         ),
-    )(query_in[0], key_in[0], value_in[0], grad_out[0], long_filter[0], short_taps[0])
-    return (layer_out[None], passed_grads[None], filter_grad[None], tap_grads[None])
+    )(query_in[0], key_in[0], value_in[0], grad_out[0], long_filter[0],
+      short_taps[0].reshape(9, 1, C))
+    specs = [
+        pl.BlockSpec((R // 4, C), lambda n: (n, 0)),
+        pl.BlockSpec((3, R // 4, C), lambda n: (0, n, 0)),
+        pl.BlockSpec((R // 4, C // G), lambda n: (n, 0)),
+        pl.BlockSpec((9, 1, C // 4), lambda n: (0, 0, n)),
+    ]
+    layer_out, passed_grads, filter_grad, tap_grads = pl.pallas_call(
+        copy_kernel,
+        grid=(4,),
+        in_specs=specs,
+        out_specs=specs,
+        out_shape=[
+            jax.ShapeDtypeStruct((R, C), bf16),
+            jax.ShapeDtypeStruct((3, R, C), bf16),
+            jax.ShapeDtypeStruct((R, C // G), f32),
+            jax.ShapeDtypeStruct((9, 1, C), f32),
+        ],
+    )(layer_out, passed_grads, filter_grad, tap_grads)
+    tap_grads = tap_grads.reshape(1, 3, 3, C)
+    return (layer_out[None], passed_grads[None], filter_grad[None], tap_grads)
 
 
 def solution(mesh):

time: 120 us -> 96.9 us (0.81)
  the two profiles are of different devices: /device:TPU:1 before, /device:TPU:64 now
where the time goes in v3:
time: 96.9 us; the launch traced here: 96.7 us
  Pallas kernels  96.1 us (99%)
    pallas_call x1, Pallas kernels, local(): pl.pallas_call(whole_kernel, in_specs=[hbm] * 4 + [vmem] * 2, out_specs=[...  91.2 us
    pallas_call x1, Pallas kernels, local(): pl.pallas_call(copy_kernel, grid=(4,), in_specs=specs, out_specs=specs, o...  4.83 us

profile of v3, /device:TPU:64, one launch (start us, length us, event | category | flops | bytes accessed | tf_op | source)
XLA Modules:
  0.0 96.7 jit_solution(15927488792772281039)
XLA Ops:
  0.6 91.2 %shard_map.93 = (bf16[128,4096]{1,0:T(8,128)(2,1)}, bf16[3,128,4096]{2,1,0:T(8,128)(2,1)}, f32[128,256]{1,0:T(8,128)}, f32[9,1,4096]{2,1,0:T(1,128)}) custom-call(bf16[128,4096]{1,0:T(8,128)(2,1)} %bitcast.10, bf16[128,4096]{1,0:T(8,128)(2,1)} %bitcast.11, bf16[128,4096]{1,0:T(8,128)(2,1)} %bitcast.12, bf16[128,4096]{1,0:T(8,128)(2,1)} %bitcast.13, ...), custom_call_target="tpu_custom_call" | custom-call | tf_op jit(solution)/shard_map/pallas_call | solution.py:541
  91.9 4.8 %shard_map.94 = (bf16[128,4096]{1,0:T(8,128)(2,1)}, bf16[3,128,4096]{2,1,0:T(8,128)(2,1)}, f32[128,256]{1,0:T(8,128)}, f32[9,1,4096]{2,1,0:T(1,128)}) custom-call(bf16[128,4096]{1,0:T(8,128)(2,1)} %get-tuple-element.12.out_in, bf16[3,128,4096]{2,1,0:T(8,128)(2,1)} %get-tuple-element.13.passed_in, f32[128,256]{1,0:T(8,128)} %get-tuple-element.14.fgrad_in, ...), custom_call_target="tpu_custom_call" | custom-call | tf_op jit(solution)/shard_map/pallas_call | solution.py:603

commit v4 on v3

--- a/solution.py
+++ b/solution.py
@@ -44,17 +44,18 @@
     return taps[0] * x + taps[1] * back1 + taps[2] * back2
 
 
-def features(lanes, in_refs, halo_ref, taps_ref):
+def features(lanes, in_refs, halo, taps_ref):
     out = []
     for w in range(3):
         x = in_refs[w][:, lanes].astype(f32)
         taps = [taps_ref[3 * w + j, :, lanes] for j in range(3)]
-        out.append(
-            short_filter(
-                x, halo_ref[2 * w : 2 * w + 1, lanes], halo_ref[2 * w + 1 : 2 * w + 2, lanes], taps
-            )
-        )
+        out.append(short_filter(x, halo[2 * w : 2 * w + 1], halo[2 * w + 1 : 2 * w + 2], taps))
     return out
+
+
+def eight_rows(ref, b):
+    rows = ref[...].astype(f32)
+    return jnp.where(b == 0, rows[0:8], rows[8:16])
 
 
 def build_base(h, base_ref):
@@ -133,7 +134,7 @@
     q_hbm, k_hbm, v_hbm, g_hbm, filter_ref, taps_ref,
     out_hbm, passed_ref, fgrad_ref, tap_ref,
     inputs, out_ref, feat, send, recv, ret_send, ret_recv, band, base, gram, fold, slabs, zeros,
-    halo_out, halo_in, edge_out, edge_in, filt_pack, filt_out, filt_in, fg_out, fg_in, fg_rows,
+    halo_pack, halo_out, halo_in, edge_pack, edge_out, edge_in, filt_pack, filt_out, filt_in, fg_out, fg_in, fg_rows,
     tap_out, tap_in, sum_out, sum_in,
     s_halo, r_halo, s_filt, r_filt, s_fwd, r_fwd, s_ret, r_ret, s_edge, r_edge,
     s_pipe, r_pipe, s_fg, r_fg, s_tap, r_tap, s_sum, r_sum, s_zero, s_in, s_out,
@@ -151,7 +152,8 @@
         load(w).start()
 
     def peer_of(s):
-        return lax.rem(me + s, N)
+        half = lax.div(s + 1, 2)
+        return lax.rem(me + N + half * (2 * lax.rem(s, 2) - 1), N)
 
     def each_peer(fn):
         def step(s, carry):
@@ -194,10 +196,28 @@
 
     for w in range(4):
         load(w).wait()
+    halo_pack[...] = jnp.zeros_like(halo_pack)
     for w in range(3):
-        last = raw[w][R - 16 : R, :].astype(f32)
-        halo_out[2 * w : 2 * w + 2, :] = last[14:16]
-    halo_out[6:8, :] = jnp.zeros((2, C), f32)
+        last = raw[w][R - 16 : R, :].astype(f32)[14:16]
+        for q in range(Q):
+            for b in range(B):
+                first = q * CQ + b * W
+                halo_pack[q, 8 * b + 2 * w : 8 * b + 2 * w + 2, :] = last[:, first : first + W]
+    halo_out[...] = halo_pack[...].astype(bf16)
+
+    pl.semaphore_wait(barrier, N + 1)
+
+    def halo_copy(q):
+        return remote(
+            halo_out.at[q], halo_in.at[q], s_halo.at[q], r_halo.at[q],
+            {"seq": jnp.minimum(me + 1, N - 1)},
+        )
+
+    @pl.when(me < N - 1)
+    def _():
+        for q in range(Q):
+            halo_copy(q).start()
+
     turned = filter_ref[...].T
     for k in range(N):
         for q in range(Q):
@@ -205,21 +225,6 @@
             filt_pack[k, q * GQ : (q + 1) * GQ, :] = turned[first : first + GQ]
     filt_out[...] = filt_pack[...].astype(bf16)
     filt_in[me] = filt_out[me]
-
-    pl.semaphore_wait(barrier, N + 1)
-
-    def halo_copy(q):
-        lanes = block(q, CQ)
-        return remote(
-            halo_out.at[:, lanes], halo_in.at[:, lanes], s_halo.at[q], r_halo.at[q],
-            {"seq": jnp.minimum(me + 1, N - 1)},
-        )
-
-    @pl.when(me < N - 1)
-    def _():
-        for q in range(Q):
-            halo_copy(q).start()
-
     filt = spread(filt_out, filt_in, s_filt, r_filt)
     each_peer(filt[0])
 
@@ -241,7 +246,7 @@
         def step(b, carry):
             n = q * B + b
             lanes = block(n, W)
-            query, keyed, valued = features(lanes, raw, halo_in, taps_ref)
+            query, keyed, valued = features(lanes, raw, eight_rows(halo_in.at[q], b), taps_ref)
             feat[0, :, lanes] = query
             feat[1, :, lanes] = keyed
             feat[2, :, lanes] = valued
@@ -321,11 +326,12 @@
             grads = (grad * conv, back * feat[2, :, lanes], back * feat[1, :, lanes])
             for w in range(3):
                 feat[w, :, lanes] = grads[w]
-                edge_out[q, 2 * w : 2 * w + 2, block(b, W)] = grads[w][0:2]
-            edge_out[q, 6:8, block(b, W)] = jnp.zeros((2, W), f32)
+            rows = [g[0:2] for g in grads] + [jnp.zeros((2, W), f32)]
+            edge_pack[block(b, 8), :] = jnp.concatenate(rows, axis=0)
             return carry
 
         lax.fori_loop(0, B, step, 0)
+        edge_out[q] = edge_pack[...].astype(bf16)
 
         out_copy(q).start()
 
@@ -335,7 +341,7 @@
 
         @pl.when(me == N - 1)
         def _():
-            edge_in[q] = jnp.zeros((8, CQ), f32)
+            edge_in[q] = jnp.zeros((16, W), bf16)
 
     def tap(half):
         return spread(tap_out.at[half], tap_in.at[half], s_tap.at[half], r_tap.at[half])
@@ -355,10 +361,11 @@
             n = q * B + b
             lanes = block(n, W)
             near = block(b, W)
+            edge = eight_rows(edge_in.at[q], b)
             for w in range(3):
                 g0 = feat[w, :, lanes]
-                g1 = rows_up(g0, edge_in[q, 2 * w : 2 * w + 1, near])
-                g2 = rows_up(g1, edge_in[q, 2 * w + 1 : 2 * w + 2, near])
+                g1 = rows_up(g0, edge[2 * w : 2 * w + 1])
+                g2 = rows_up(g1, edge[2 * w + 1 : 2 * w + 2])
                 x = raw[w][:, lanes].astype(f32)
                 total = None
                 for j, g in enumerate((g0, g1, g2)):
@@ -479,34 +486,33 @@
 
     lax.fori_loop(0, Q + LAG + 1, step, 0)
 
-    sum_phase(1)
-    fgrad_phase()
-    for half in range(HALVES):
-        each_peer(lambda k: sum_copy(half, k, k).wait_recv())
-        for k in range(N):
-            first = half * (C // HALVES) + k * TW
-            for r in range(9):
-                tap_ref[r, :, first : first + TW] = sum_in[half, k, r : r + 1, :]
-
-    @pl.when(me < N - 1)
-    def _():
-        for q in range(Q):
-            halo_copy(q).wait_send()
-
-    each_peer(filt[2])
-
     def sent(q, carry):
         each_peer(fwd(q)[2])
         each_peer(ret(q)[2])
         out_copy(q).wait()
         return carry
 
-    lax.fori_loop(0, Q, sent, 0)
+    fgrad_phase()
+    lax.fori_loop(0, Q // 2, sent, 0)
+    sum_phase(1)
+    lax.fori_loop(Q // 2, Q, sent, 0)
+
+    @pl.when(me < N - 1)
+    def _():
+        for q in range(Q):
+            halo_copy(q).wait_send()
+
+    each_peer(filt[2])
     each_peer(fg_wait_send)
     for half in range(HALVES):
         each_peer(tap(half)[2])
         each_peer(lambda k: sum_copy(half, k, k).wait_send())
 
+    for half in range(HALVES):
+        each_peer(lambda k: sum_copy(half, k, k).wait_recv())
+        for r in range(9):
+            tap_ref[r, half * N : (half + 1) * N, :] = sum_in[half, :, r, :]
+
     @pl.when(me > 0)
     def _():
         for q in range(Q):
@@ -527,11 +533,24 @@
         zero_copy().wait()
 
 
-def copy_kernel(out_in, passed_in, fgrad_in, tap_in, out, passed, fgrad, tap):
-    out[...] = out_in[...]
-    passed[...] = passed_in[...]
-    fgrad[...] = fgrad_in[...]
-    tap[...] = tap_in[...]
+def copy_kernel(
+    out_in, passed_in, fgrad_in, tap_in, out, passed, fgrad, tap, v_out, v_passed, v_fgrad, v_tap, sem
+):
+    pairs = []
+    for n in range(4):
+        rows = slice(n * R // 4, (n + 1) * R // 4)
+        pairs += [(passed_in.at[w, rows], v_passed.at[w, rows], passed.at[w, rows]) for w in range(3)]
+        pairs.append((out_in.at[rows], v_out.at[rows], out.at[rows]))
+    pairs += [(fgrad_in, v_fgrad, fgrad), (tap_in, v_tap, tap)]
+    into = [pltpu.make_async_copy(a, b, sem.at[0, i]) for i, (a, b, _) in enumerate(pairs)]
+    back = [pltpu.make_async_copy(b, c, sem.at[1, i]) for i, (_, b, c) in enumerate(pairs)]
+    for copy in into:
+        copy.start()
+    for first, second in zip(into, back):
+        first.wait()
+        second.start()
+    for copy in back:
+        copy.wait()
 
 
 def local(query_in, key_in, value_in, grad_out, long_filter, short_taps):
@@ -546,7 +565,7 @@
             jax.ShapeDtypeStruct((R, C), bf16),
             jax.ShapeDtypeStruct((3, R, C), bf16),
             jax.ShapeDtypeStruct((R, C // G), f32),
-            jax.ShapeDtypeStruct((9, 1, C), f32),
+            jax.ShapeDtypeStruct((9, C // TW, TW), f32),
         ],
         scratch_shapes=[
             pltpu.VMEM((4, R, C), bf16),
@@ -562,10 +581,12 @@
             pltpu.VMEM((Q * GQ, 8, T), f32),
             pltpu.VMEM((Q, 3, R, CQ), bf16),
             pltpu.VMEM((3, R, C), bf16),
-            pltpu.VMEM((8, C), f32),
-            pltpu.VMEM((8, C), f32),
-            pltpu.VMEM((Q, 8, CQ), f32),
-            pltpu.VMEM((Q, 8, CQ), f32),
+            pltpu.VMEM((Q, 16, W), f32),
+            pltpu.VMEM((Q, 16, W), bf16),
+            pltpu.VMEM((Q, 16, W), bf16),
+            pltpu.VMEM((16, W), f32),
+            pltpu.VMEM((Q, 16, W), bf16),
+            pltpu.VMEM((Q, 16, W), bf16),
             pltpu.VMEM((N, Q * GQ, R), f32),
             pltpu.VMEM((N, Q * GQ, R), bf16),
             pltpu.VMEM((N, Q * GQ, R), bf16),
@@ -594,23 +615,24 @@
         ),
     )(query_in[0], key_in[0], value_in[0], grad_out[0], long_filter[0],
       short_taps[0].reshape(9, 1, C))
-    specs = [
-        pl.BlockSpec((R // 4, C), lambda n: (n, 0)),
-        pl.BlockSpec((3, R // 4, C), lambda n: (0, n, 0)),
-        pl.BlockSpec((R // 4, C // G), lambda n: (n, 0)),
-        pl.BlockSpec((9, 1, C // 4), lambda n: (0, 0, n)),
-    ]
     layer_out, passed_grads, filter_grad, tap_grads = pl.pallas_call(
         copy_kernel,
-        grid=(4,),
-        in_specs=specs,
-        out_specs=specs,
+        in_specs=[hbm] * 4,
+        out_specs=[hbm] * 4,
         out_shape=[
             jax.ShapeDtypeStruct((R, C), bf16),
             jax.ShapeDtypeStruct((3, R, C), bf16),
             jax.ShapeDtypeStruct((R, C // G), f32),
-            jax.ShapeDtypeStruct((9, 1, C), f32),
+            jax.ShapeDtypeStruct((9, C // TW, TW), f32),
         ],
+        scratch_shapes=[
+            pltpu.VMEM((R, C), bf16),
+            pltpu.VMEM((3, R, C), bf16),
+            pltpu.VMEM((R, C // G), f32),
+            pltpu.VMEM((9, C // TW, TW), f32),
+            dma((2, 18)),
+        ],
+        compiler_params=pltpu.CompilerParams(vmem_limit_bytes=60 * 2**20),
     )(layer_out, passed_grads, filter_grad, tap_grads)
     tap_grads = tap_grads.reshape(1, 3, 3, C)
     return (layer_out[None], passed_grads[None], filter_grad[None], tap_grads)

time: 96.9 us -> 90.7 us (0.936)
  the two profiles are of different devices: /device:TPU:64 before, /device:TPU:1 now
where the time goes in v4:
time: 90.7 us; the launch traced here: 90.5 us
  Pallas kernels  89.9 us (99%)
    pallas_call x1, Pallas kernels, local(): pl.pallas_call(whole_kernel, in_specs=[hbm] * 4 + [vmem] * 2, out_specs=[...  85.8 us
    pallas_call x1, Pallas kernels, local(): pl.pallas_call(copy_kernel, in_specs=[hbm] * 4, out_specs=[hbm] * 4, out_...  4.11 us

profile of v4, /device:TPU:1, one launch (start us, length us, event | category | flops | bytes accessed | tf_op | source)
XLA Modules:
  0.0 90.5 jit_solution(1533519286852563785)
XLA Ops:
  0.6 85.8 %shard_map.93 = (bf16[128,4096]{1,0:T(8,128)(2,1)}, bf16[3,128,4096]{2,1,0:T(8,128)(2,1)}, f32[128,256]{1,0:T(8,128)}, f32[9,32,128]{2,1,0:T(8,128)}) custom-call(bf16[128,4096]{1,0:T(8,128)(2,1)} %bitcast.10, bf16[128,4096]{1,0:T(8,128)(2,1)} %bitcast.11, bf16[128,4096]{1,0:T(8,128)(2,1)} %bitcast.12, bf16[128,4096]{1,0:T(8,128)(2,1)} %bitcast.13, ...), custom_call_target="tpu_custom_call" | custom-call | tf_op jit(solution)/shard_map/pallas_call | solution.py:560
  86.4 4.1 %shard_map.94 = (bf16[128,4096]{1,0:T(8,128)(2,1)}, bf16[3,128,4096]{2,1,0:T(8,128)(2,1)}, f32[128,256]{1,0:T(8,128)}, f32[9,32,128]{2,1,0:T(8,128)}) custom-call(bf16[128,4096]{1,0:T(8,128)(2,1)} %get-tuple-element.12.out_in, bf16[3,128,4096]{2,1,0:T(8,128)(2,1)} %get-tuple-element.13.passed_in, f32[128,256]{1,0:T(8,128)} %get-tuple-element.14.fgrad_in, ...), custom_call_target="tpu_custom_call" | custom-call | tf_op jit(solution)/shard_map/pallas_call | solution.py:618

commit v5 on v4

--- a/solution.py
+++ b/solution.py
@@ -160,7 +160,7 @@
             fn(peer_of(s))
             return carry
 
-        lax.fori_loop(1, N, step, 0)
+        lax.fori_loop(1, N, step, 0, unroll=True)
 
     def remote(src, dst, s_sem, r_sem, where):
         return pltpu.make_async_remote_copy(
@@ -478,7 +478,7 @@
         def _():
             input_phase(t - LAG - 1)
 
-        @pl.when(t == Q // HALVES + LAG + 1)
+        @pl.when(t == Q)
         def _():
             sum_phase(0)
 

time: 90.7 us -> 90.3 us (level)
  no operation moved by 1% of the time
where the time goes in v5:
time: 90.3 us; the launch traced here: 90.2 us
  Pallas kernels  89.5 us (99%)
    pallas_call x1, Pallas kernels, local(): pl.pallas_call(whole_kernel, in_specs=[hbm] * 4 + [vmem] * 2, out_specs=[...  85.4 us
    pallas_call x1, Pallas kernels, local(): pl.pallas_call(copy_kernel, in_specs=[hbm] * 4, out_specs=[hbm] * 4, out_...  4.11 us

profile of v5, /device:TPU:1, one launch (start us, length us, event | category | flops | bytes accessed | tf_op | source)
XLA Modules:
  0.0 90.2 jit_solution(991175292829103914)
XLA Ops:
  0.6 85.4 %shard_map.93 = (bf16[128,4096]{1,0:T(8,128)(2,1)}, bf16[3,128,4096]{2,1,0:T(8,128)(2,1)}, f32[128,256]{1,0:T(8,128)}, f32[9,32,128]{2,1,0:T(8,128)}) custom-call(bf16[128,4096]{1,0:T(8,128)(2,1)} %bitcast.10, bf16[128,4096]{1,0:T(8,128)(2,1)} %bitcast.11, bf16[128,4096]{1,0:T(8,128)(2,1)} %bitcast.12, bf16[128,4096]{1,0:T(8,128)(2,1)} %bitcast.13, ...), custom_call_target="tpu_custom_call" | custom-call | tf_op jit(solution)/shard_map/pallas_call | solution.py:560
  86.1 4.1 %shard_map.94 = (bf16[128,4096]{1,0:T(8,128)(2,1)}, bf16[3,128,4096]{2,1,0:T(8,128)(2,1)}, f32[128,256]{1,0:T(8,128)}, f32[9,32,128]{2,1,0:T(8,128)}) custom-call(bf16[128,4096]{1,0:T(8,128)(2,1)} %get-tuple-element.12.out_in, bf16[3,128,4096]{2,1,0:T(8,128)(2,1)} %get-tuple-element.13.passed_in, f32[128,256]{1,0:T(8,128)} %get-tuple-element.14.fgrad_in, ...), custom_call_target="tpu_custom_call" | custom-call | tf_op jit(solution)/shard_map/pallas_call | solution.py:618

commit v6 on v5

--- a/solution.py
+++ b/solution.py
@@ -450,13 +450,13 @@
         def _():
             conv_phase(t)
 
+        @pl.when((t >= LAG) & (t < Q + LAG))
+        def _():
+            grad_phase(t - LAG)
+
         @pl.when(t + AHEAD < Q)
         def _():
             feature_phase(t + AHEAD)
-
-        @pl.when((t >= LAG) & (t < Q + LAG))
-        def _():
-            grad_phase(t - LAG)
 
         @pl.when(t + 1 < Q)
         def _():

time: 90.3 us -> 90.3 us (level)
  no operation moved by 1% of the time
where the time goes in v6:
time: 90.3 us; the launch traced here: 90.1 us
  Pallas kernels  89.5 us (99%)
    pallas_call x1, Pallas kernels, local(): pl.pallas_call(whole_kernel, in_specs=[hbm] * 4 + [vmem] * 2, out_specs=[...  85.4 us
    pallas_call x1, Pallas kernels, local(): pl.pallas_call(copy_kernel, in_specs=[hbm] * 4, out_specs=[hbm] * 4, out_...  4.11 us

profile of v6, /device:TPU:1, one launch (start us, length us, event | category | flops | bytes accessed | tf_op | source)
XLA Modules:
  0.0 90.1 jit_solution(8175927310073543857)
XLA Ops:
  0.6 85.4 %shard_map.93 = (bf16[128,4096]{1,0:T(8,128)(2,1)}, bf16[3,128,4096]{2,1,0:T(8,128)(2,1)}, f32[128,256]{1,0:T(8,128)}, f32[9,32,128]{2,1,0:T(8,128)}) custom-call(bf16[128,4096]{1,0:T(8,128)(2,1)} %bitcast.10, bf16[128,4096]{1,0:T(8,128)(2,1)} %bitcast.11, bf16[128,4096]{1,0:T(8,128)(2,1)} %bitcast.12, bf16[128,4096]{1,0:T(8,128)(2,1)} %bitcast.13, ...), custom_call_target="tpu_custom_call" | custom-call | tf_op jit(solution)/shard_map/pallas_call | solution.py:560
  86.0 4.1 %shard_map.94 = (bf16[128,4096]{1,0:T(8,128)(2,1)}, bf16[3,128,4096]{2,1,0:T(8,128)(2,1)}, f32[128,256]{1,0:T(8,128)}, f32[9,32,128]{2,1,0:T(8,128)}) custom-call(bf16[128,4096]{1,0:T(8,128)(2,1)} %get-tuple-element.12.out_in, bf16[3,128,4096]{2,1,0:T(8,128)(2,1)} %get-tuple-element.13.passed_in, f32[128,256]{1,0:T(8,128)} %get-tuple-element.14.fgrad_in, ...), custom_call_target="tpu_custom_call" | custom-call | tf_op jit(solution)/shard_map/pallas_call | solution.py:618
